TPU v7x, 32 devices: a whole 2x2x4 slice. The times are simulated.
32 devices in a mesh: grp: 2 (over x), lon: 16 (over z, y, core).
Axes of the slice: x: 2, y: 2, z: 4, core: 2. Of those that a mesh axis runs over, the one named last changes fastest.
Arguments:
- tokens: bfloat16 [8, 48, 192, 192], P('grp', None, 'lon'), parts along dimension 0, may hold values from -6 to 6
- qkv_weight: bfloat16 [192, 576], replicated, may hold values from -25 to 25
- proj_weight: bfloat16 [192, 192], replicated, may hold values from -0.4375 to 0.4375
- bias_table: float32 [16, 6, 3312], replicated, may hold values from -4 to 4
- bias_index: int32 [144, 144], replicated, may hold values from 0 to 3311, as said below
- norm_gain1: float32 [192], replicated, may hold values from 0.1 to 1.9
- norm_gain2: float32 [192], replicated, may hold values from 0.1 to 1.9
- mlp_in: bfloat16 [192, 768], replicated, may hold values from -0.4375 to 0.4375
- mlp_out: bfloat16 [768, 192], replicated, may hold values from -0.21875 to 0.21875
Outputs:
- block_out: bfloat16 [8, 48, 192, 192], P('grp', None, 'lon'), parts along dimension 0
There are 2 independent parts, one for each index of `grp`. A program takes and returns all parts, laid end to end along the dimension named above; an argument that names none is the same for every part. Nothing has to cross between parts.
Inputs may be any that keep to these rules, and one draw needn't show every extreme that they name: bias_index[i, j] is the bias table's row for query position i and key position j; pairs with the same level pair, the same row pair and the same column offset share a row, and every row is used.
All inputs are finite; a program needn't handle non-finite values.
Results may differ from a plain program's by a relative error of at most 0.011.
Values may be sent and summed in bfloat16 or wider, within the bound.
No kernel may reach another device: no remote copies, remote signals or barrier semaphores. Data moves between devices by JAX's collectives and lax.ppermute only.
A program may use at most 256 MiB of HBM per device.

v0:
```python
import jax
import jax.numpy as jnp
from jax import lax
from jax.sharding import PartitionSpec as P


def shifted_2(value, axis, steps):
    count = lax.axis_size(axis)
    pairs = [(source, (source + steps) % count) for source in range(count)]
    return lax.ppermute(value, axis, pairs)


def region_grid(levels, lat_rows):
    level_ids = jnp.arange(levels, dtype=jnp.int32)
    zone_level = jnp.where(level_ids < levels - 2, 0, jnp.where(level_ids < levels - 1, 1, 2))
    row_ids = jnp.arange(lat_rows, dtype=jnp.int32)
    zone_row = jnp.where(row_ids < lat_rows - 6, 0, jnp.where(row_ids < lat_rows - 3, 1, 2))
    return (zone_level[:, None] * 3 + zone_row[None, :]).astype(jnp.int32)


def to_windows(field_grid, columns):
    levels, lat_rows, longitude, features = field_grid.shape
    window_count = longitude // columns
    pieces = field_grid.reshape(levels // 2, 2, lat_rows // 6, 6, window_count, columns, features)
    return pieces.transpose(0, 2, 4, 1, 3, 5, 6).reshape(
        levels // 2, lat_rows // 6, window_count, 12 * columns, features
    )


def from_windows(blocked, columns):
    level_windows, row_windows, window_count, positions, features = blocked.shape
    pieces = blocked.reshape(level_windows, row_windows, window_count, 2, 6, columns, features)
    return pieces.transpose(0, 3, 1, 4, 2, 5, 6).reshape(
        level_windows * 2, row_windows * 6, window_count * columns, features
    )


def window_zones(levels, lat_rows, columns):
    zone_ids = (
        region_grid(levels, lat_rows)
        .reshape(levels // 2, 2, lat_rows // 6, 6)
        .transpose(0, 2, 1, 3)
    )
    zone_ids = jnp.broadcast_to(zone_ids[..., None], (levels // 2, lat_rows // 6, 2, 6, columns))
    return zone_ids.reshape(levels // 2, lat_rows // 6, 12 * columns)


def layer_norm(values):
    average = jnp.mean(values, axis=-1, keepdims=True)
    centred = values - average
    spread = jnp.mean(centred * centred, axis=-1, keepdims=True)
    return centred * lax.rsqrt(spread + 1e-05)


def attend(queries, keys_values, index_rows, earth_table, query_columns, head_count):
    levels, lat_rows, unused, channels = queries.shape
    head_size = channels // head_count
    query_windows = to_windows(queries, query_columns)
    window_count = query_windows.shape[2]
    query_windows = query_windows.reshape(
        levels // 2, lat_rows // 6, window_count, 12 * query_columns, head_count, head_size
    )
    pair_windows = to_windows(keys_values, 12).reshape(
        levels // 2, lat_rows // 6, window_count, 144, 2, head_count, head_size
    )
    zone_query = window_zones(levels, lat_rows, query_columns)
    zone_key = window_zones(levels, lat_rows, 12)
    table_levels = earth_table.reshape(levels // 2, lat_rows // 6, head_count, -1)
    scaling = head_size ** (-0.5)

    def one_level(blocked):
        query_block, pair_block, table_block, query_zone, key_zone = blocked
        earth_bias = jnp.take(table_block, index_rows, axis=2).transpose(0, 2, 1, 3, 4)
        scores = (
            jnp.einsum(
                "tnqhd,tnkhd->tnhqk",
                query_block,
                pair_block[:, :, :, 0],
                preferred_element_type=jnp.float32,
            )
            * scaling
            + earth_bias
        )
        allowed = query_zone[:, None, None, :, None] == key_zone[:, None, None, None, :]
        scores = jnp.where(allowed, scores, -1000000000.0)
        highest = jnp.max(scores, axis=-1, keepdims=True)
        weights = jnp.exp(scores - highest)
        probabilities = (weights / jnp.sum(weights, axis=-1, keepdims=True)).astype(jnp.bfloat16)
        context = jnp.einsum(
            "tnhqk,tnkhd->tnqhd",
            probabilities,
            pair_block[:, :, :, 1],
            preferred_element_type=jnp.float32,
        )
        return context.astype(jnp.bfloat16)

    context = lax.map(one_level, (query_windows, pair_windows, table_levels, zone_query, zone_key))
    context = context.reshape(
        levels // 2, lat_rows // 6, window_count, 12 * query_columns, channels
    )
    return from_windows(context, query_columns)


def per_device(
    tokens, qkv_weight, proj_weight, bias_table, bias_index, norm_gain1, norm_gain2, mlp_in, mlp_out
):
    channels = tokens.shape[3]
    head_count = bias_table.shape[1]
    shifted = jnp.roll(tokens, (-1, -3), axis=(0, 1))
    arrived = shifted_2(shifted[:, :, :6], "lon", -1)
    framed = jnp.concatenate([shifted[:, :, 6:], arrived], axis=2)
    projected = jnp.dot(framed, qkv_weight, preferred_element_type=jnp.float32).astype(jnp.bfloat16)
    context = attend(
        projected[..., :channels],
        projected[..., channels:],
        bias_index[None],
        bias_table,
        12,
        head_count,
    )
    attended_frame = jnp.dot(context, proj_weight, preferred_element_type=jnp.float32).astype(
        jnp.bfloat16
    )
    returned = shifted_2(attended_frame[:, :, 6:], "lon", 1)
    attended = jnp.concatenate([returned, attended_frame[:, :, :6]], axis=2)
    attended = jnp.roll(attended, (1, 3), axis=(0, 1))
    middle = (
        tokens.astype(jnp.float32) + norm_gain1 * layer_norm(attended.astype(jnp.float32))
    ).astype(jnp.bfloat16)
    expanded = jax.nn.gelu(
        jnp.dot(middle, mlp_in, preferred_element_type=jnp.float32), approximate=False
    ).astype(jnp.bfloat16)
    reduced = jnp.dot(expanded, mlp_out, preferred_element_type=jnp.float32)
    return (middle.astype(jnp.float32) + norm_gain2 * layer_norm(reduced)).astype(jnp.bfloat16)


def solution(mesh):
    placed = (P("grp", None, "lon", None), P(), P(), P(), P(), P(), P(), P(), P())
    return jax.shard_map(
        per_device,
        mesh=mesh,
        in_specs=placed,
        out_specs=P("grp", None, "lon", None),
        check_vma=False,
    )
```

profile of v0, /device:TPU:0, one launch (start us, length us, event | category | flops | bytes accessed | tf_op | source)
XLA Modules:
  0.0 440.6 jit_solution(12843402711509337148)
XLA Ops:
  3.0 5.5 %collective-permute-start = (bf16[4,48,6,192]{3,1,2,0:T(8,128)(2,1)S(1)}, bf16[4,48,6,192]{3,1,2,0:T(8,128)(2,1)S(1)}, u32[]{:S(2)}, u32[]{:S(2)}) collective-permute-start(bf16[4,48,6,192]{3,1,2,0:T(8,128)(2,1)S(1)} %get-tuple-element.98), channel_id=1, source_target_pairs={{0,15},{1,0},{2,1},{3,2},{4,3},{5,4},{6,5},{7,6},{8,7},{9,8},{10,9... | collective-permute-start | bytes 1327112 | tf_op jit(solution)/shard_map/ppermute | solution.py:10
  8.8 7.1 %collective-permute-done = bf16[4,48,6,192]{3,1,2,0:T(8,128)(2,1)S(1)} collective-permute-done((bf16[4,48,6,192]{3,1,2,0:T(8,128)(2,1)S(1)}, bf16[4,48,6,192]{3,1,2,0:T(8,128)(2,1)S(1)}, u32[]{:S(2)}, u32[]{:S(2)}) %collective-permute-start) | collective-permute-done | bytes 442400 | tf_op jit(solution)/shard_map/ppermute | solution.py:10
  18.6 1.4 copy.32
  19.9 2.2 reshape.175
  22.2 2.1 copy.33
  24.3 8.8 %reshape_reshape.9 = bf16[2,8,1,144,2,6,32]{6,5,4,1,3,0,2:T(8,128)(2,1)} reshape(bf16[2,8,1,2,6,12,384]{6,1,5,4,3,0,2:T(8,128)(2,1)S(1)} %copy.33) | data formatting | bytes 3538944 | tf_op jit(solution)/shard_map/reshape;reshape | solution.py:63
  33.1 11.9 %copy.36 = bf16[2,8,1,144,2,6,32]{3,6,5,1,4,2,0:T(8,128)(2,1)} copy(bf16[2,8,1,144,2,6,32]{6,5,4,1,3,0,2:T(8,128)(2,1)} %reshape_reshape.9) | data formatting | bytes 3538944 | tf_op jit(solution)/shard_map/while | solution.py:97
  47.6 3.7 reshape_reshape.10
  51.2 6.8 %copy.37 = bf16[2,8,1,144,6,32]{3,5,4,1,2,0:T(8,128)(2,1)} copy(bf16[2,8,1,144,6,32]{5,4,1,3,0,2:T(8,128)(2,1)} %reshape_reshape.10) | data formatting | bytes 1769472 | tf_op jit(solution)/shard_map/while | solution.py:97
  58.0 329.4 %while.11 = (s32[]{:T(128)}, bf16[2,8,1,144,6,32]{3,5,4,1,2,0:T(8,128)(2,1)}, bf16[2,8,1,144,2,6,32]{3,6,5,1,4,2,0:T(8,128)(2,1)}, s32[2,8,144]{2,1,0:T(8,128)S(...) while((s32[]{:T(128)}, ...), condition=%wide.region_3.4_spmd, body=%wide.region_0.3_spmd.sunk | while | flops 136962336 | bytes 69840248 | solution.py:97
  70.5 7.3 %copy.55 = f32[1,8,6,3312]{2,1,3,0:T(8,128)} copy(f32[1,8,6,3312]{3,1,0,2:T(8,128)S(1)} %constant_dynamic-slice_fusion.2) | data formatting | bytes 1271808 | tf_op jit(solution)/shard_map/while/body/jit(dynamic_index_in_dim)/dynamic_slice | solution.py:97
  78.0 51.2 %gather_fusion = f32[20736,8,6]{2,1,0:T(8,128)} fusion(f32[8,6,3312]{1,0,2:T(8,128)} %bitcast.111, s32[21504]{0:T(1024)S(1)} %pad_clamp_fusion.2), kind=kCustom, calls=%fused_computation.clone.1 | custom fusion | bytes 8045568 | tf_op jit(solution)/shard_map/while/body/eval_jaxpr/jit(_take)/gather | solution.py:73
  129.2 81.5 %copy.56 = f32[144,144,8,6]{0,1,3,2:T(8,128)} copy(f32[144,144,8,6]{3,2,1,0:T(8,128)} %bitcast.110) | data formatting | bytes 7962624 | tf_op jit(solution)/shard_map/while/body/eval_jaxpr/jit(_take)/gather | solution.py:73
  210.7 1.6 dynamic-slice_bitcast_fusion.5
  212.7 5.1 %fusion.96 = f32[8,6,144,144]{2,3,1,0:T(8,128)S(1)} fusion(f32[144,144,8,6]{0,1,3,2:T(8,128)} %copy.56, pred[144,144]{0,1:T(8,128)(4,1)S(1)} %copy.57, pred[8,144,144]{1,2,0:T(8,128)(4,1)S(1)} %broadcast_compare_fusion.2, bf16[8,1,144,2,6,32]{2,5,4,0,3,1:T(8,128)(2,1)S(1)} %dynamic-slice_bitcast_fusion.5, ...), kind=kOutput, calls=%fused_computation.3.clone.1 | convolution fusion | flops 67682304 | bytes 12964352 | tf_op jit(solution)/shard_map/while/body/eval_jaxpr/tnqhd,tnkhd->tnhqk/dot_general | solution.py:75
  217.8 1.4 fusion.97
  219.2 1.5 copy-done.1
  220.7 7.6 %fusion.98 = bf16[2,8,1,144,6,32]{3,5,4,1,2,0:T(8,128)(2,1)} fusion(bf16[2,8,1,144,6,32]{3,5,4,1,2,0:T(8,128)(2,1)} %get-tuple-element.154, s32[]{:T(128)} %get-tuple-element.153, f32[8,6,144]{2,1,0:T(8,128)S(1)} %fusion.97, bf16[8,1,144,2,6,32]{2,5,4,0,3,1:T(8,128)(2,1)S(1)} %dynamic-slice_bitcast_fusion.5, f32[8,6,144,144]{2,3,1,0:T(8,128)} %copy-done.1), kind=kOutput, calls=%fused_computation.10.clone.1 | convolution fusion | flops 66915216 | bytes 15794688 | tf_op jit(solution)/shard_map/while/body/eval_jaxpr/tnhqk,tnkhd->tnqhd/dot_general | solution.py:89
  229.5 7.3 %copy.55 = f32[1,8,6,3312]{2,1,3,0:T(8,128)} copy(f32[1,8,6,3312]{3,1,0,2:T(8,128)S(1)} %constant_dynamic-slice_fusion.2) | data formatting | bytes 1271808 | tf_op jit(solution)/shard_map/while/body/jit(dynamic_index_in_dim)/dynamic_slice | solution.py:97
  237.0 51.2 %gather_fusion = f32[20736,8,6]{2,1,0:T(8,128)} fusion(f32[8,6,3312]{1,0,2:T(8,128)} %bitcast.111, s32[21504]{0:T(1024)S(1)} %pad_clamp_fusion.2), kind=kCustom, calls=%fused_computation.clone.1 | custom fusion | bytes 8045568 | tf_op jit(solution)/shard_map/while/body/eval_jaxpr/jit(_take)/gather | solution.py:73
  288.2 81.5 %copy.56 = f32[144,144,8,6]{0,1,3,2:T(8,128)} copy(f32[144,144,8,6]{3,2,1,0:T(8,128)} %bitcast.110) | data formatting | bytes 7962624 | tf_op jit(solution)/shard_map/while/body/eval_jaxpr/jit(_take)/gather | solution.py:73
  369.7 1.6 dynamic-slice_bitcast_fusion.5
  371.7 5.1 %fusion.96 = f32[8,6,144,144]{2,3,1,0:T(8,128)S(1)} fusion(f32[144,144,8,6]{0,1,3,2:T(8,128)} %copy.56, pred[144,144]{0,1:T(8,128)(4,1)S(1)} %copy.57, pred[8,144,144]{1,2,0:T(8,128)(4,1)S(1)} %broadcast_compare_fusion.2, bf16[8,1,144,2,6,32]{2,5,4,0,3,1:T(8,128)(2,1)S(1)} %dynamic-slice_bitcast_fusion.5, ...), kind=kOutput, calls=%fused_computation.3.clone.1 | convolution fusion | flops 67682304 | bytes 12964352 | tf_op jit(solution)/shard_map/while/body/eval_jaxpr/tnqhd,tnkhd->tnhqk/dot_general | solution.py:75
  376.8 1.4 fusion.97
  378.3 1.5 copy-done.1
  379.7 7.7 %fusion.98 = bf16[2,8,1,144,6,32]{3,5,4,1,2,0:T(8,128)(2,1)} fusion(bf16[2,8,1,144,6,32]{3,5,4,1,2,0:T(8,128)(2,1)} %get-tuple-element.154, s32[]{:T(128)} %get-tuple-element.153, f32[8,6,144]{2,1,0:T(8,128)S(1)} %fusion.97, bf16[8,1,144,2,6,32]{2,5,4,0,3,1:T(8,128)(2,1)S(1)} %dynamic-slice_bitcast_fusion.5, f32[8,6,144,144]{2,3,1,0:T(8,128)} %copy-done.1), kind=kOutput, calls=%fused_computation.10.clone.1 | convolution fusion | flops 66915216 | bytes 15794688 | tf_op jit(solution)/shard_map/while/body/eval_jaxpr/tnhqk,tnkhd->tnqhd/dot_general | solution.py:89
  387.4 8.2 %copy.39 = bf16[2,8,1,144,6,32]{5,4,1,3,0,2:T(8,128)(2,1)} copy(bf16[2,8,1,144,6,32]{3,5,4,1,2,0:T(8,128)(2,1)} %get-tuple-element.62) | data formatting | bytes 1769472 | tf_op jit(solution)/shard_map/while | solution.py:97
  395.6 5.4 %reshape_reshape.11 = bf16[2,8,1,2,6,12,192]{6,1,5,4,3,0,2:T(8,128)(2,1)S(1)} reshape(bf16[2,8,1,144,6,32]{5,4,1,3,0,2:T(8,128)(2,1)} %copy.39) | data formatting | bytes 1769472 | tf_op jit(solution)/shard_map/reshape;reshape | solution.py:32
  404.1 12.2 %collective-permute-done.1 = bf16[4,48,6,192]{3,1,2,0:T(8,128)(2,1)S(1)} collective-permute-done((bf16[4,48,6,192]{3,1,2,0:T(8,128)(2,1)S(1)}, bf16[4,48,6,192]{3,1,2,0:T(8,128)(2,1)S(1)}, u32[]{:S(2)}, u32[]{:S(2)}) %collective-permute-start.1) | collective-permute-done | bytes 442400 | tf_op jit(solution)/shard_map/ppermute | solution.py:10
  417.6 3.0 fusion.20
  420.6 16.5 %fusion.83 = (f32[4,48,12]{1,2,0:T(8,128)S(1)}, f32[4,48,12,192]{3,1,2,0:T(8,128)S(1)}) fusion(bf16[768,192]{0,1:T(8,128)(2,1)S(1)} %copy-done.8, f32[4,48,12,768]{3,1,2,0:T(8,128)S(1)} %get-tuple-element.99, u16[4,48,768]{2,1,0:T(8,128)(2,1)S(1)} %get-tuple-element.78, u16[4,48,768]{2,1,0:T(8,128)(2,1)S(1)} %get-tuple-element.77), kind=kOutput, calls=%fused_computation.128 | convolution fusion | flops 803780352 | bytes 9741312 | tf_op jit(solution)/shard_map/dot_general | solution.py:133
  437.9 2.5 add_convert_fusion
  (66 shorter events, 16.9 us)
Async XLA Ops:
  0.0 417.6 %copy-start = (bf16[192,768]{1,0:T(8,128)(2,1)S(1)}, bf16[192,768]{1,0:T(8,128)(2,1)}, u32[]{:S(2)}) copy-start(bf16[192,768]{1,0:T(8,128)(2,1)} %param.18) | copy-start | bytes 884740
  2.6 13.3 %copy-start.9 = (bf16[192,576]{1,0:T(8,128)(2,1)S(1)}, bf16[192,576]{1,0:T(8,128)(2,1)}, u32[]{:S(2)}) copy-start(bf16[192,576]{1,0:T(8,128)(2,1)} %param.12) | copy-start | bytes 663556
  3.0 12.9 %collective-permute-start = (bf16[4,48,6,192]{3,1,2,0:T(8,128)(2,1)S(1)}, bf16[4,48,6,192]{3,1,2,0:T(8,128)(2,1)S(1)}, u32[]{:S(2)}, u32[]{:S(2)}) collective-permute-start(bf16[4,48,6,192]{3,1,2,0:T(8,128)(2,1)S(1)} %get-tuple-element.98), channel_id=1, source_target_pairs={{0,15},{1,0},{2,1},{3,2},{4,3},{5,4},{6,5},{7,6},{8,7},{9,8},{10,9... | collective-permute-start | bytes 1327112 | tf_op jit(solution)/shard_map/ppermute | solution.py:10
  17.0 1.6 copy-start.3
  33.1 11.9 %slice-start = ((bf16[4,48,12,576]{3,1,2,0:T(8,128)(2,1)}), bf16[4,48,12,192]{3,1,2,0:T(8,128)(2,1)S(1)}, s32[]{:S(2)}) async-start(bf16[4,48,12,576]{3,1,2,0:T(8,128)(2,1)} %copy-done.3), calls=%async_computation | async-start | bytes 2359296 | tf_op jit(solution)/shard_map/slice | solution.py:114
  51.2 6.8 %copy-start.2 = (s32[144,144]{1,0:T(8,128)S(1)}, s32[144,144]{1,0:T(8,128)}, u32[]{:S(2)}) copy-start(s32[144,144]{1,0:T(8,128)} %param.15) | copy-start | bytes 248836
  217.8 2.9 copy-start.1
  376.8 2.9 copy-start.1
  401.0 2.1 copy-start.5
  403.6 14.0 %copy-start.4 = (bf16[4,48,12,192]{3,1,2,0:T(8,128)(2,1)S(1)}, bf16[4,48,12,192]{3,1,2,0:T(8,128)(2,1)}, u32[]{:S(2)}) copy-start(bf16[4,48,12,192]{3,1,2,0:T(8,128)(2,1)} %param.11) | copy-start | bytes 2654212
  403.6 14.0 %copy-start.6 = (f32[192]{0:T(256)S(1)}, f32[192]{0:T(256)}, u32[]{:S(2)}) copy-start(f32[192]{0:T(256)} %param.16) | copy-start | bytes 2308
  403.7 12.6 %collective-permute-start.1 = (bf16[4,48,6,192]{3,1,2,0:T(8,128)(2,1)S(1)}, bf16[4,48,6,192]{3,1,2,0:T(8,128)(2,1)S(1)}, u32[]{:S(2)}, u32[]{:S(2)}) collective-permute-start(bf16[4,48,6,192]{3,1,2,0:T(8,128)(2,1)S(1)} %get-tuple-element.95), channel_id=1, source_target_pairs={{0,1},{1,2},{2,3},{3,4},{4,5},{5,6},{6,7},{7,8},{8,9},{9,10},{10,1... | collective-permute-start | bytes 1327112 | tf_op jit(solution)/shard_map/ppermute | solution.py:10
  417.6 3.0 copy-start.8
  420.6 17.3 %copy-start.7 = (f32[192]{0:T(256)S(1)}, f32[192]{0:T(256)}, u32[]{:S(2)}) copy-start(f32[192]{0:T(256)} %param.17) | copy-start | bytes 2308
where the time goes:
time: 445 us; the launch traced here: 441 us
  local copies, waits for them, and re-layouts  348 us (78%)
  matrix products  46.5 us (10%)
  waiting for transfers between devices  19.3 us (4%)
  loops' own time  11.5 us (3%)
  other arithmetic  8.67 us (2%)
  starting transfers between devices  5.96 us (1%)
    gather x4, local copies, waits for them, and re-layouts, one_level(): jnp.take(table_block, index_rows, axis=2).transpose(0, 2, 1, 3, 4)  265 us
    while x3, local copies, waits for them, and re-layouts, attend(): lax.map(one_level, (query_windows, pair_windows, table_levels, zone_query...  26.9 us
    ppermute x2, waiting for transfers between devices, shifted_2(): return lax.ppermute(value, axis, pairs)  19.3 us
    dynamic_slice x4, local copies, waits for them, and re-layouts, attend(): lax.map(one_level, (query_windows, pair_windows, table_levels, zone_query...  16.9 us
    dot_general x1, matrix products, per_device(): reduced = jnp.dot(expanded, mlp_out, preferred_element_type=jnp.float32)  16.5 us
    dot_general x2, matrix products, one_level(): jnp.einsum('tnhqk,tnkhd->tnqhd', probabilities, pair_block[:, :, :, 1], p...  15.3 us
    another operation x1, loops' own time, attend(): lax.map(one_level, (query_windows, pair_windows, table_levels, zone_query...  11.5 us
    dot_general x2, matrix products, one_level(): jnp.einsum('tnqhd,tnkhd->tnhqk', query_block, pair_block[:, :, :, 0], pre...  10.2 us
  transfers between devices with their start and end apart: 2, of which 2 were waited for; matrix products, arithmetic and copies ran while one was open for 0% of the time, Pallas kernels for 0%

commit v1 on v0

v1 whole, which is shorter than its diff:
```python
import functools
import math

import jax
import jax.numpy as jnp
import numpy as np
from jax import lax
from jax.experimental import pallas as pl
from jax.experimental.pallas import tpu as pltpu
from jax.sharding import PartitionSpec as P

LOG2E = math.log2(math.e)
NEG = -1.0e9 * LOG2E
NT = (((1,), (1,)), ((), ()))
NN = (((1,), (0,)), ((), ()))
HEADS = 6
GROUP = 72
LANES = 512
F32 = jnp.float32
BF16 = jnp.bfloat16


def mm(a, b, dims=NN):
    return lax.dot_general(a, b, dims, preferred_element_type=F32)


PAIR_TILES = ((0,), (0, 1), (1, 2), (2, 0))
TILE_PAIRS = ((3, 0, 1), (1, 2), (2, 3))


def pair_rows(pair):
    out = []
    for w in range(2):
        for slot in range(12):
            for r in range(6):
                out.append((slot, (6 * (2 * pair + w) + r + 3) % 48))
    return out


def pack_matrices():
    mats = []
    for pair in range(4):
        tiles = PAIR_TILES[pair]
        m = np.zeros((144, 192 * len(tiles)), np.float32)
        for k, (slot, a) in enumerate(pair_rows(pair)):
            m[k, 192 * tiles.index(a // 16) + slot * 16 + a % 16] = 1.0
        mats.append(m)
    return np.concatenate(mats, axis=1)


def unpack_matrices():
    mats = []
    for tile in range(3):
        pairs = TILE_PAIRS[tile]
        m = np.zeros((192, 144 * len(pairs)), np.float32)
        for n, pair in enumerate(pairs):
            for k, (slot, a) in enumerate(pair_rows(pair)):
                if a // 16 == tile:
                    m[slot * 16 + a % 16, 144 * n + k] = 1.0
        mats.append(np.pad(m, ((0, 0), (0, 432 - m.shape[1]))))
    return np.stack(mats)


def pick_matrix():
    m = np.zeros((GROUP, LANES), np.float32)
    for h in range(HEADS):
        for q in range(GROUP):
            m[q, h * GROUP + q] = 1.0
    return m


def pack_kernel(tok, mats, west, east):
    for wz in range(2):
        zs = ((2 * wz + 1) % 4, (2 * wz + 2) % 4)
        for half, out in ((0, west), (1, east)):
            tiles = []
            for j in range(3):
                tiles.append(
                    jnp.concatenate(
                        [tok[z, 6 * half + c, 16 * j : 16 * j + 16, :] for c in range(6) for z in zs], axis=0
                    )
                )
            at = 0
            for pair in range(4):
                total = None
                for j in PAIR_TILES[pair]:
                    part = mm(mats[:, at : at + 192], tiles[j])
                    total = part if total is None else total + part
                    at += 192
                out[pl.ds((wz * 4 + pair) * 144, 144), :] = total.astype(BF16)


def prep_kernel(tab, idx, bias, tab_t, rows):
    count = tab.shape[1]
    for k in range(0, count, 128):
        n = min(128, count - k)
        tab_t[k : k + n, 0:96] = (tab[:, k : k + n] * LOG2E).T
    lane = lax.broadcasted_iota(jnp.int32, (16, LANES), 1)
    sub = lax.broadcasted_iota(jnp.int32, (16, LANES), 0)
    place = lane % GROUP
    slot = lane % 12
    lq_is1 = slot >= 6
    rq_hi = (slot % 6) >= 3
    last_level = sub >= 8
    last_row = (sub % 8) == 7

    def body(kr, carry):
        j0 = kr * 12
        for m in range(4):
            for c in range(6):
                if m == 0:
                    cq, ck = 0, (12 - c if c else 11)
                elif m == 1:
                    cq, ck = 0, 6 - c
                else:
                    cq, ck = 6 * (m - 2) + c, 0
                for e in range(12):
                    r = idx[e * 12 + cq, j0 + ck]
                    rows[m, c * 12 + e : c * 12 + e + 1, :] = tab_t[pl.ds(r, 1), :]
        xs = []
        for m in range(4):
            t = rows[m].T
            xs.append(
                jnp.concatenate(
                    [t[16 * h : 16 * h + 16, :] for h in range(HEADS)]
                    + [jnp.zeros((16, LANES - HEADS * GROUP), F32)],
                    axis=1,
                )
            )
        prev = [pltpu.roll(x, LANES - GROUP, 1) for x in xs]
        lk_is1 = kr >= 6
        rk_hi = (kr % 6) >= 3
        bad = (last_level & (lq_is1 != lk_is1)) | (last_row & (rq_hi != rk_hi))
        for s in range(2):
            for ck in range(12):
                u, v = divmod(ck, 6)
                m = 3 - s - u
                if v == 0:
                    row = xs[m]
                else:
                    keep = (place < GROUP - 12 * v) & (lane < HEADS * GROUP)
                    row = pltpu.roll(jnp.where(keep, xs[m], prev[m - 1]), 12 * v, 1)
                row = jnp.where(bad, NEG, row)
                for k in range(LANES // 128):
                    bias[k, pl.ds(s * 144 + ck * 12 + kr, 16, stride=288), :] = row[:, 128 * k : 128 * k + 128]
        return carry

    lax.fori_loop(0, 12, body, 0)


def norm(values):
    average = jnp.mean(values, axis=-1, keepdims=True)
    centred = values - average
    spread = jnp.mean(centred * centred, axis=-1, keepdims=True)
    return centred * lax.rsqrt(spread + 1e-05)


def main_kernel(
    own_w, own_e, halo_w, halo_e, bias, wq, wk, wv_t, wp, gain1, gain2, w_in, w_out, pick, unmat, out, done
):
    step = pl.program_id(0)
    wz = step // 4
    pair = step % 4
    channel = lax.broadcasted_iota(jnp.int32, (GROUP, 192), 1)
    lane = lax.broadcasted_iota(jnp.int32, (32, LANES), 1)
    owns, contexts = [], []
    for s in range(2):
        own_ref, halo_ref = ((own_w, halo_w), (own_e, halo_e))[s]
        own = own_ref[...]
        own32 = own.astype(F32)
        halo32 = halo_ref[...].astype(F32)
        owns.append(own32)
        q2 = mm(own, wq[...]) * (LOG2E / math.sqrt(32.0))
        for t in range(2):
            a, b = own32[GROUP * t : GROUP * (t + 1)], halo32[GROUP * t : GROUP * (t + 1)]
            window = jnp.concatenate([b, a] if s == 0 else [a, b], axis=0).astype(BF16)
            keys = mm(window, wk[...]).astype(BF16)
            values_t = mm(wv_t[...], window, NT).astype(BF16)
            values_t = jnp.concatenate([values_t, jnp.ones((16, 144), BF16)], axis=0)
            q = q2[GROUP * t : GROUP * (t + 1)]
            blocks = [
                jnp.where((channel >= 32 * h) & (channel < 32 * h + 32), q, 0.0) for h in range(HEADS)
            ] + [jnp.zeros((LANES - HEADS * GROUP, 192), F32)]
            queries = jnp.concatenate(blocks, axis=0).astype(BF16)
            first = 288 * t + 144 * s
            offset = jnp.concatenate([bias[k, first : first + 144, :] for k in range(LANES // 128)], axis=1)
            scores = mm(keys, queries, NT) + offset
            scores = jnp.where(offset < -1.0e8, NEG, scores)
            highest = jnp.max(scores, axis=0, keepdims=True)
            weights = jnp.exp2(scores - highest).astype(BF16)
            mixed = mm(values_t, weights)
            inverse = 1.0 / mixed[192:193]
            diag = jnp.concatenate(
                [
                    jnp.where(
                        (lane >= GROUP * h) & (lane < GROUP * h + GROUP), mixed[32 * h : 32 * h + 32] * inverse, 0.0
                    )
                    for h in range(HEADS)
                ],
                axis=0,
            ).astype(BF16)
            contexts.append(mm(pick[...], diag, NT))
    context = jnp.concatenate(contexts, axis=0).astype(BF16)
    own32 = jnp.concatenate(owns, axis=0)
    attended = mm(context, wp[...]).astype(BF16).astype(F32)
    middle = (own32 + gain1[...] * norm(attended)).astype(BF16)
    hidden = mm(middle, w_in[...])
    expanded = (0.5 * hidden * (1.0 + lax.erf(hidden * (1.0 / math.sqrt(2.0))))).astype(BF16)
    reduced = mm(expanded, w_out[...])
    result = (middle.astype(F32) + gain2[...] * norm(reduced)).astype(BF16)
    done[0, pl.ds(pl.multiple_of(pair * 144, 144), 144), :] = result[:144]
    done[1, pl.ds(pl.multiple_of(pair * 144, 144), 144), :] = result[144:]

    @pl.when(pair == 3)
    def _():
        for half in range(2):
            for j in range(3):
                pairs = TILE_PAIRS[j]
                if j == 0:
                    rows = jnp.concatenate([done[half, 432:576, :], done[half, 0:288, :]], axis=0)
                else:
                    rows = done[half, 144 * pairs[0] : 144 * pairs[0] + 288, :]
                back = mm(unmat[j, :, : 144 * len(pairs)], rows).astype(BF16)
                for c in range(6):
                    for level in range(2):
                        k = 2 * c + level
                        z = lax.rem(2 * wz + 1 + level, 4)
                        out[z, 6 * half + c, 16 * j : 16 * j + 16, :] = back[16 * k : 16 * k + 16]


def shifted_by(value, axis, steps):
    count = lax.axis_size(axis)
    return lax.ppermute(value, axis, [(i, (i + steps) % count) for i in range(count)])


def per_device(
    tokens, qkv_weight, proj_weight, bias_table, bias_index, norm_gain1, norm_gain2, mlp_in, mlp_out
):
    levels, lat, strip, channels = tokens.shape
    types, heads, count = bias_table.shape
    tok = tokens.transpose(0, 2, 1, 3)
    vmem = pl.BlockSpec(memory_space=pltpu.VMEM)
    half_shape = jax.ShapeDtypeStruct((types * GROUP, channels), BF16)
    west, east = pl.pallas_call(
        pack_kernel,
        out_shape=(half_shape, half_shape),
        in_specs=[vmem, vmem],
        out_specs=(vmem, vmem),
        name="pack",
    )(tok, jnp.asarray(pack_matrices(), BF16))
    halo_w = shifted_by(east, "lon", 1)
    halo_e = shifted_by(west, "lon", -1)
    table = bias_table.transpose(1, 0, 2).reshape(heads * types, count)
    bias = pl.pallas_call(
        prep_kernel,
        out_shape=jax.ShapeDtypeStruct((LANES // 128, types * 288, 128), F32),
        in_specs=[vmem, pl.BlockSpec(memory_space=pltpu.SMEM)],
        out_specs=vmem,
        scratch_shapes=[pltpu.VMEM((3328, 128), F32), pltpu.VMEM((4, GROUP, 128), F32)],
        compiler_params=pltpu.CompilerParams(vmem_limit_bytes=40 * 1024 * 1024),
        cost_estimate=pl.CostEstimate(flops=20_000_000_000, bytes_accessed=12_000_000, transcendentals=0),
        name="bias_prep",
    )(table, bias_index)

    def whole(*shape):
        return pl.BlockSpec(shape, lambda i: (0,) * len(shape))

    strip_spec = pl.BlockSpec((2 * GROUP, channels), lambda i: (i, 0))
    hidden = mlp_in.shape[1]
    out = pl.pallas_call(
        main_kernel,
        grid=(types // 2,),
        out_shape=jax.ShapeDtypeStruct((levels, strip, lat, channels), BF16),
        in_specs=[strip_spec] * 4
        + [
            pl.BlockSpec((LANES // 128, 576, 128), lambda i: (0, i, 0)),
            whole(channels, channels),
            whole(channels, channels),
            whole(channels, channels),
            whole(channels, channels),
            whole(1, channels),
            whole(1, channels),
            whole(channels, hidden),
            whole(hidden, channels),
            whole(GROUP, LANES),
            whole(3, 192, 432),
        ],
        out_specs=whole(levels, strip, lat, channels),
        scratch_shapes=[pltpu.VMEM((2, 576, channels), BF16)],
        compiler_params=pltpu.CompilerParams(vmem_limit_bytes=40 * 1024 * 1024),
        name="block",
    )(
        west,
        east,
        halo_w,
        halo_e,
        bias,
        qkv_weight[:, :channels],
        qkv_weight[:, channels : 2 * channels],
        qkv_weight[:, 2 * channels :].T,
        proj_weight,
        norm_gain1[None],
        norm_gain2[None],
        mlp_in,
        mlp_out,
        jnp.asarray(pick_matrix(), BF16),
        jnp.asarray(unpack_matrices(), BF16),
    )
    return out.transpose(0, 2, 1, 3)


def solution(mesh):
    placed = (P("grp", None, "lon", None), P(), P(), P(), P(), P(), P(), P(), P())
    return jax.shard_map(
        per_device,
        mesh=mesh,
        in_specs=placed,
        out_specs=P("grp", None, "lon", None),
        check_vma=False,
    )
```

time: 445 us -> 72.5 us (0.16)
  local copies, waits for them, and re-layouts: 348 us -> 17.8 us
  Pallas kernels: 0 us -> 48.7 us
  matrix products: 46.5 us -> 0 us
  waiting for transfers between devices: 19.3 us -> 0.01 us
  loops' own time: 11.5 us -> 0 us
  other arithmetic: 8.67 us -> 0 us
    gather x4 -> x0, local copies, waits for them, and re-layouts: 265 us -> none  [one_level(): jnp.take(table_block, index_rows, axis=2).transpose(0, 2, 1, 3, 4)]
    pallas_call x0 -> x3, Pallas kernels: none -> 48.7 us  [the longest x1 27.7 us: per_device(): pl.pallas_call(main_kernel, grid=(types // 2,), out_shape=jax.ShapeDtypeS...]
    dot_general x8 -> x0, matrix products: 46.5 us -> none  [the longest x1 16.5 us: per_device(): reduced = jnp.dot(expanded, mlp_out, preferred_element_type=jnp.float32)]
    while x7 -> x0, local copies, waits for them, and re-layouts: 29.8 us -> none  [the longest x3 26.9 us: attend(): lax.map(one_level, (query_windows, pair_windows, table_levels, zone_query...]
    ppermute x2, waiting for transfers between devices: 19.3 us -> 0.01 us  [shifted_by(): lax.ppermute(value, axis, [(i, (i + steps) % count) for i in range(count)])]
    another operation x3 -> x0, local copies, waits for them, and re-layouts: 17.9 us -> none  [the longest x1 8.84 us: attend(): to_windows(keys_values, 12)]
    dynamic_slice x4 -> x0, local copies, waits for them, and re-layouts: 16.9 us -> none  [attend(): lax.map(one_level, (query_windows, pair_windows, table_levels, zone_query...]
    another operation x1 -> x0, loops' own time: 11.5 us -> none  [attend(): lax.map(one_level, (query_windows, pair_windows, table_levels, zone_query...]
  transfers between devices with their start and end apart: 2 -> 2, of which waited for: 2 -> 0; matrix products, arithmetic and copies ran while one was open for 0% -> 5% of each run, Pallas kernels for 0% -> 25%
where the time goes in v1:
time: 72.5 us; the launch traced here: 72.1 us
  Pallas kernels  48.7 us (67%)
  local copies, waits for them, and re-layouts  17.8 us (25%)
  starting transfers between devices  5.45 us (8%)
    pallas_call x1, Pallas kernels, per_device(): pl.pallas_call(main_kernel, grid=(types // 2,), out_shape=jax.ShapeDtypeS...  27.7 us
    pallas_call x1, Pallas kernels, per_device(): pl.pallas_call(prep_kernel, out_shape=jax.ShapeDtypeStruct((LANES // 128,...  18 us
    unnamed x32, local copies, waits for them, and re-layouts  11.9 us
    ppermute x2, starting transfers between devices, shifted_by(): lax.ppermute(value, axis, [(i, (i + steps) % count) for i in range(count)])  5.45 us
    pallas_call x2, local copies, waits for them, and re-layouts, per_device(): pl.pallas_call(pack_kernel, out_shape=(half_shape, half_shape), in_specs=...  3.21 us
    pallas_call x1, Pallas kernels, per_device(): pl.pallas_call(pack_kernel, out_shape=(half_shape, half_shape), in_specs=...  2.99 us
    ppermute x2, local copies, waits for them, and re-layouts, shifted_by(): lax.ppermute(value, axis, [(i, (i + steps) % count) for i in range(count)])  2.6 us
  transfers between devices with their start and end apart: 2, of which 0 were waited for; matrix products, arithmetic and copies ran while one was open for 5% of the time, Pallas kernels for 25%

profile of v1, /device:TPU:0, one launch (start us, length us, event | category | flops | bytes accessed | tf_op | source)
XLA Modules:
  0.0 72.1 jit_solution(15598339111975315045)
XLA Ops:
  0.0 3.0 %pack.1 = (bf16[1152,192]{1,0:T(8,128)(2,1)}, bf16[1152,192]{1,0:T(8,128)(2,1)}) custom-call(bf16[4,12,48,192]{3,2,1,0:T(8,128)(2,1)} %bitcast.12, bf16[144,1344]{1,0:T(8,128)(2,1)} %constant.6.clone.mats), custom_call_target="tpu_custom_call" | custom-call | tf_op jit(solution)/shard_map/pack/pallas_call | solution.py:244
  3.0 2.2 %copy.15 = bf16[1152,192]{0,1:T(8,128)(2,1)} copy(bf16[1152,192]{1,0:T(8,128)(2,1)} %get-tuple-element.8.own_e) | data formatting | bytes 884736 | tf_op jit(solution)/shard_map/pack/pallas_call | solution.py:244
  5.2 0.5 collective-permute-start
  5.7 0.0 copy-done.2
  5.7 1.0 %copy.16 = bf16[1152,192]{0,1:T(8,128)(2,1)} copy(bf16[1152,192]{1,0:T(8,128)(2,1)S(1)} %copy-done.2) | data formatting | bytes 884736 | tf_op jit(solution)/shard_map/pack/pallas_call | solution.py:244
  6.7 5.0 %collective-permute-start.1 = (bf16[1152,192]{0,1:T(8,128)(2,1)}, bf16[1152,192]{0,1:T(8,128)(2,1)}, u32[]{:S(2)}, u32[]{:S(2)}) collective-permute-start(bf16[1152,192]{0,1:T(8,128)(2,1)} %copy.16), channel_id=1, source_target_pairs={{0,15},{1,0},{2,1},{3,2},{4,3},{5,4},{6,5},{7,6},{8,7},{9,8},{10,9... | collective-permute-start | bytes 1327112 | tf_op jit(solution)/shard_map/ppermute | solution.py:233
  11.7 0.0 copy-done.11
  11.7 0.0 copy-done.12
  11.7 18.0 %bias_prep.1.bias = f32[4,4608,128]{2,1,0:T(8,128)S(1)} custom-call(f32[96,3312]{1,0:T(8,128)S(1)} %bitcast.11, s32[144,144]{1,0:T(8,128)S(1)} %copy-done.12), custom_call_target="tpu_custom_call" | custom-call | flops 20000000000 | bytes 12000000 | tf_op jit(solution)/shard_map/bias_prep/pallas_call | solution.py:254
  29.7 0.0 copy-start
  29.7 3.7 %copy-done = f32[4,4608,128]{2,1,0:T(8,128)} copy-done((f32[4,4608,128]{2,1,0:T(8,128)}, f32[4,4608,128]{2,1,0:T(8,128)S(1)}, u32[]{:S(2)}) %copy-start) | copy-done | bytes 9437208
  33.3 0.0 copy-done.13
  33.3 0.1 fusion
  33.5 0.7 %copy.21 = bf16[192,192]{0,1:T(8,128)(2,1)} copy(bf16[192,192]{1,0:T(8,128)(2,1)S(1)} %get-tuple-element.9) | data formatting | bytes 147456
  34.2 0.0 copy-done.14
  34.2 0.0 copy-start.10
  34.2 0.2 copy.20.w_out
  34.4 0.0 collective-permute-done
  34.4 1.4 %copy.18.halo_w = bf16[1152,192]{1,0:T(8,128)(2,1)S(1)} copy(bf16[1152,192]{0,1:T(8,128)(2,1)} %collective-permute-done) | data formatting | bytes 884736 | tf_op jit(solution)/shard_map/ppermute | solution.py:233
  35.8 0.0 collective-permute-done.1
  35.8 1.2 %copy.19.halo_e = bf16[1152,192]{1,0:T(8,128)(2,1)S(1)} copy(bf16[1152,192]{0,1:T(8,128)(2,1)} %collective-permute-done.1) | data formatting | bytes 884736 | tf_op jit(solution)/shard_map/ppermute | solution.py:233
  37.0 0.0 copy-done.3
  37.0 0.0 copy-done.4
  37.0 0.0 copy-done.9
  37.0 0.0 copy-done.10
  37.1 0.0 copy-start.1
  37.1 3.7 %copy-done.1 = f32[4,4608,128]{2,1,0:T(8,128)S(1)} copy-done((f32[4,4608,128]{2,1,0:T(8,128)S(1)}, f32[4,4608,128]{2,1,0:T(8,128)}, u32[]{:S(2)}) %copy-start.1) | copy-done | bytes 9437208
  40.7 0.9 %copy-done.5 = bf16[192,192]{0,1:T(8,128)(2,1)S(1)} copy-done((bf16[192,192]{0,1:T(8,128)(2,1)S(1)}, bf16[192,192]{0,1:T(8,128)(2,1)}, u32[]{:S(2)}) %copy-start.5) | copy-done | bytes 73752
  41.6 1.0 %copy-done.6 = bf16[192,768]{1,0:T(8,128)(2,1)S(1)} copy-done((bf16[192,768]{1,0:T(8,128)(2,1)S(1)}, bf16[192,768]{1,0:T(8,128)(2,1)}, u32[]{:S(2)}) %copy-start.6) | copy-done | bytes 294936
  42.6 0.9 %copy-done.7 = bf16[192,192]{1,0:T(8,128)(2,1)S(1)} copy-done((bf16[192,192]{1,0:T(8,128)(2,1)S(1)}, bf16[192,192]{1,0:T(8,128)(2,1)}, u32[]{:S(2)}) %copy-start.7) | copy-done | bytes 73752
  43.5 0.9 %copy-done.8 = bf16[72,512]{1,0:T(8,128)(2,1)S(1)} copy-done((bf16[72,512]{1,0:T(8,128)(2,1)S(1)}, bf16[72,512]{1,0:T(8,128)(2,1)}, u32[]{:S(2)}) %copy-start.8) | copy-done | bytes 73752
  44.4 27.7 %block.1 = bf16[4,12,48,192]{3,2,1,0:T(8,128)(2,1)} custom-call(bf16[1152,192]{1,0:T(8,128)(2,1)S(1)} %copy-done.2, bf16[1152,192]{1,0:T(8,128)(2,1)S(1)} %copy-done.3, bf16[1152,192]{1,0:T(8,128)(2,1)S(1)} %copy.18.halo_w, bf16[1152,192]{1,0:T(8,128)(2,1)S(1)} %copy.19.halo_e, f32[4,4608,128]{2,1,0:T(8,128)S(1)} %copy-done.1, ...), custom_call_target="tpu_custom_call" | custom-call | tf_op jit(solution)/shard_map/block/pallas_call | solution.py:270
  (12 shorter events, 0.0 us)
Async XLA Ops:
  3.0 2.7 %copy-start.2 = (bf16[1152,192]{1,0:T(8,128)(2,1)S(1)}, bf16[1152,192]{1,0:T(8,128)(2,1)}, u32[]{:S(2)}) copy-start(bf16[1152,192]{1,0:T(8,128)(2,1)} %get-tuple-element.7.own_w) | copy-start | bytes 1327108
  3.0 8.7 %copy-start.11 = (f32[16,6,3312]{2,0,1:T(8,128)S(1)}, f32[16,6,3312]{2,0,1:T(8,128)}, u32[]{:S(2)}) copy-start(f32[16,6,3312]{2,0,1:T(8,128)} %param.15) | copy-start | bytes 3815428
  3.0 8.7 %copy-start.12 = (s32[144,144]{1,0:T(8,128)S(1)}, s32[144,144]{1,0:T(8,128)}, u32[]{:S(2)}) copy-start(s32[144,144]{1,0:T(8,128)} %idx.1) | copy-start | bytes 248836
  5.2 29.2 %collective-permute-start = (bf16[1152,192]{0,1:T(8,128)(2,1)}, bf16[1152,192]{0,1:T(8,128)(2,1)}, u32[]{:S(2)}, u32[]{:S(2)}) collective-permute-start(bf16[1152,192]{0,1:T(8,128)(2,1)} %copy.15), channel_id=1, source_target_pairs={{0,1},{1,2},{2,3},{3,4},{4,5},{5,6},{6,7},{7,8},{8,9},{9,10},{10,1... | collective-permute-start | bytes 1327112 | tf_op jit(solution)/shard_map/ppermute | solution.py:233
  6.7 29.1 %collective-permute-start.1 = (bf16[1152,192]{0,1:T(8,128)(2,1)}, bf16[1152,192]{0,1:T(8,128)(2,1)}, u32[]{:S(2)}, u32[]{:S(2)}) collective-permute-start(bf16[1152,192]{0,1:T(8,128)(2,1)} %copy.16), channel_id=1, source_target_pairs={{0,15},{1,0},{2,1},{3,2},{4,3},{5,4},{6,5},{7,6},{8,7},{9,8},{10,9... | collective-permute-start | bytes 1327112 | tf_op jit(solution)/shard_map/ppermute | solution.py:233
  11.7 21.7 %copy-start.13 = (bf16[192,576]{1,0:T(8,128)(2,1)S(1)}, bf16[192,576]{1,0:T(8,128)(2,1)}, u32[]{:S(2)}) copy-start(bf16[192,576]{1,0:T(8,128)(2,1)} %param.13) | copy-start | bytes 663556
  11.7 22.5 %copy-start.14 = (bf16[768,192]{0,1:T(8,128)(2,1)S(1)}, bf16[768,192]{0,1:T(8,128)(2,1)}, u32[]{:S(2)}) copy-start(bf16[768,192]{0,1:T(8,128)(2,1)} %param.20) | copy-start | bytes 884740
  29.7 3.7 %copy-start = (f32[4,4608,128]{2,1,0:T(8,128)}, f32[4,4608,128]{2,1,0:T(8,128)S(1)}, u32[]{:S(2)}) copy-start(f32[4,4608,128]{2,1,0:T(8,128)S(1)} %bias_prep.1.bias) | copy-start | bytes 28311556
  34.2 2.8 %copy-start.3 = (bf16[1152,192]{1,0:T(8,128)(2,1)S(1)}, bf16[1152,192]{1,0:T(8,128)(2,1)}, u32[]{:S(2)}) copy-start(bf16[1152,192]{1,0:T(8,128)(2,1)} %get-tuple-element.8.own_e) | copy-start | bytes 1327108
  34.2 2.8 %copy-start.4 = (bf16[3,192,432]{2,1,0:T(8,128)(2,1)S(1)}, bf16[3,192,432]{2,1,0:T(8,128)(2,1)}, u32[]{:S(2)}) copy-start(bf16[3,192,432]{2,1,0:T(8,128)(2,1)} %constant.8.clone.unmat) | copy-start | bytes 1492996
  34.2 2.8 %copy-start.9 = (f32[192]{0:T(256)S(1)}, f32[192]{0:T(256)}, u32[]{:S(2)}) copy-start(f32[192]{0:T(256)} %param.17) | copy-start | bytes 2308
  34.2 2.8 %copy-start.10 = (f32[192]{0:T(256)S(1)}, f32[192]{0:T(256)}, u32[]{:S(2)}) copy-start(f32[192]{0:T(256)} %param.18) | copy-start | bytes 2308
  37.1 3.7 %copy-start.1 = (f32[4,4608,128]{2,1,0:T(8,128)S(1)}, f32[4,4608,128]{2,1,0:T(8,128)}, u32[]{:S(2)}) copy-start(f32[4,4608,128]{2,1,0:T(8,128)} %copy-done) | copy-start | bytes 28311556
  40.7 0.9 %copy-start.5 = (bf16[192,192]{0,1:T(8,128)(2,1)S(1)}, bf16[192,192]{0,1:T(8,128)(2,1)}, u32[]{:S(2)}) copy-start(bf16[192,192]{0,1:T(8,128)(2,1)} %copy.21) | copy-start | bytes 221188
  41.6 1.0 %copy-start.6 = (bf16[192,768]{1,0:T(8,128)(2,1)S(1)}, bf16[192,768]{1,0:T(8,128)(2,1)}, u32[]{:S(2)}) copy-start(bf16[192,768]{1,0:T(8,128)(2,1)} %w_in.1) | copy-start | bytes 884740
  42.6 0.9 %copy-start.7 = (bf16[192,192]{1,0:T(8,128)(2,1)S(1)}, bf16[192,192]{1,0:T(8,128)(2,1)}, u32[]{:S(2)}) copy-start(bf16[192,192]{1,0:T(8,128)(2,1)} %wp.1) | copy-start | bytes 221188
  43.5 0.9 %copy-start.8 = (bf16[72,512]{1,0:T(8,128)(2,1)S(1)}, bf16[72,512]{1,0:T(8,128)(2,1)}, u32[]{:S(2)}) copy-start(bf16[72,512]{1,0:T(8,128)(2,1)} %constant.7.clone.pick) | copy-start | bytes 221188

commit v2 on v1

v2 whole, which is shorter than its diff:
```python
import math

import jax
import jax.numpy as jnp
import numpy as np
from jax import lax
from jax.experimental import pallas as pl
from jax.experimental.pallas import tpu as pltpu
from jax.sharding import PartitionSpec as P

LOG2E = math.log2(math.e)
NEG = -1.0e9 * LOG2E
NT = (((1,), (1,)), ((), ()))
NN = (((1,), (0,)), ((), ()))
HEADS = 6
GROUP = 72
TYPES = 4
LANES = 512
F32 = jnp.float32
BF16 = jnp.bfloat16


def mm(a, b, dims=NN):
    return lax.dot_general(a, b, dims, preferred_element_type=F32)


PAIR_TILES = ((0,), (0, 1), (1, 2), (2, 0))
TILE_PAIRS = ((3, 0, 1), (1, 2), (2, 3))


def pair_rows(pair):
    out = []
    for w in range(2):
        for slot in range(12):
            for r in range(6):
                out.append((slot, (6 * (2 * pair + w) + r + 3) % 48))
    return out


def pack_matrices():
    mats = []
    for pair in range(4):
        for tile in PAIR_TILES[pair]:
            m = np.zeros((144, 192), np.float32)
            for k, (slot, a) in enumerate(pair_rows(pair)):
                if a // 16 == tile:
                    m[k, slot * 16 + a % 16] = 1.0
            mats.append(m)
    return np.stack(mats)


def unpack_matrices():
    mats = []
    for tile in range(3):
        pairs = TILE_PAIRS[tile]
        m = np.zeros((192, 144 * len(pairs)), np.float32)
        for n, pair in enumerate(pairs):
            for k, (slot, a) in enumerate(pair_rows(pair)):
                if a // 16 == tile:
                    m[slot * 16 + a % 16, 144 * n + k] = 1.0
        mats.append(np.pad(m, ((0, 0), (0, 432 - m.shape[1]))))
    return np.stack(mats)


def mask_codes():
    lane = np.arange(256)[None] + np.zeros((24, 1), np.int32)
    second = np.arange(24)[:, None] >= 12
    kr = np.arange(24)[:, None] % 12
    slot = (lane % GROUP) % 12
    code = ((slot >= 6) != (kr >= 6)) * 1 + ((slot % 6 >= 3) != (kr % 6 >= 3)) * 2
    source = np.where(second, (lane + 244) % 256, lane)
    place = np.where(source < 3 * GROUP, source % GROUP, GROUP) + 12 * second
    return np.stack([code, place])


def pack_kernel(tok, mats, send_w, send_e):
    for wz in range(2):
        zs = ((2 * wz + 1) % 4, (2 * wz + 2) % 4)
        for half, send in ((0, send_w), (1, send_e)):
            tiles = [
                jnp.concatenate(
                    [tok[z, 6 * half + c, 16 * j : 16 * j + 16, :] for c in range(6) for z in zs], axis=0
                )
                for j in range(3)
            ]
            at = 0
            for pair in range(4):
                total = None
                for j in PAIR_TILES[pair]:
                    part = mm(mats[at], tiles[j])
                    total = part if total is None else total + part
                    at += 1
                piece = total.astype(BF16)
                first = 576 * wz + 144 * pair
                send[first : first + 144, :] = piece[:, :128]
                send[1152 + 144 * pair : 1296 + 144 * pair, 64 * wz : 64 * wz + 64] = piece[:, 128:]


def turn(x, by):
    half = LANES // 2
    if by % half == 0:
        return x
    return jnp.concatenate([pltpu.roll(x[:, k : k + half], by % half, 1) for k in range(0, x.shape[1], half)], axis=1)


def gather_kernel(tab, index, qkv, mlp_out_t, tables, weight, w_out, tab_t, rows, picked, idx, sem):
    numbers = index[...].astype(F32)
    turned = numbers.T
    picked[...] = jnp.concatenate(
        [numbers[12 * e : 12 * e + 1] for e in range(12)] + [turned[12 * e : 12 * e + 1] for e in range(12)], axis=0
    ).astype(jnp.int32)
    copy = pltpu.make_async_copy(picked, idx, sem)
    copy.start()
    w_out[...] = mlp_out_t[...].astype(F32).T.astype(BF16)
    whole = qkv[...].astype(F32)
    gap = jnp.zeros((192, 32), F32)
    cols = []
    for k in range(6):
        cols += [whole[:, 96 * k : 96 * k + 96], gap]
    wide = jnp.concatenate(cols, axis=1).astype(BF16)
    none = jnp.zeros((64, 768), BF16)
    for wz in range(2):
        weight[wz, 0:128, :] = wide[:128]
        weight[wz, 128 + 64 * wz : 192 + 64 * wz, :] = wide[128:]
        weight[wz, 192 - 64 * wz : 256 - 64 * wz, :] = none
    count = tab.shape[1]
    for k in range(0, count, 128):
        n = min(128, count - k)
        tab_t[k : k + n, 0:96] = (tab[:, k : k + n] * LOG2E).T
    copy.wait()
    gap = jnp.zeros((16, 40), F32)
    for kr in range(12):
        j0 = kr * 12
        for m in range(4):
            for c in range(6):
                if m == 0:
                    cq, ck = 0, (12 - c if c else 11)
                elif m == 1:
                    cq, ck = 0, 6 - c
                else:
                    cq, ck = 6 * (m - 2) + c, 0
                for e in range(12):
                    r = idx[e, j0 + ck] if m < 2 else idx[12 + kr, e * 12 + cq]
                    rows[kr, m, c * 12 + e : c * 12 + e + 1, :] = tab_t[pl.ds(r, 1), :]
            t = rows[kr, m].T
            x = jnp.concatenate(
                [t[16 * h : 16 * h + 16, :] for h in range(3)]
                + [gap]
                + [t[16 * h : 16 * h + 16, :] for h in range(3, 6)]
                + [gap],
                axis=1,
            )
            for k in range(LANES // 128):
                tables[m, k, 16 * kr : 16 * kr + 16, :] = x[:, 128 * k : 128 * k + 128]


    def variants(kr, carry):
        here = pl.ds(pl.multiple_of(16 * kr, 16), 16)
        later = pl.ds(pl.multiple_of(192 + 16 * kr, 16), 16)
        for m in range(4):
            x = jnp.concatenate([tables[m, k, here, :] for k in range(LANES // 128)], axis=1)
            moved = turn(x, -GROUP)
            pieces = [(m, later, turn(x, 12))]
            if m < 3:
                pieces += [(4 + m, here, moved), (4 + m, later, turn(moved, 12))]
            for n, at, value in pieces:
                for k in range(LANES // 128):
                    tables[n, k, at, :] = value[:, 128 * k : 128 * k + 128]
        return carry

    lax.fori_loop(0, 12, variants, 0)


def norm(values, eps):
    average = jnp.mean(values, axis=-1, keepdims=True)
    centred = values - average
    spread = jnp.mean(centred * centred, axis=-1, keepdims=True)
    return centred * lax.rsqrt(spread + eps)


def main_kernel(
    send_w, send_e, halo_w, halo_e, tables, codes, weight, wp, gain1, gain2, w_in, w_out, unmat, out, done, held, kept
):
    step = pl.program_id(0)
    steps = 16 // TYPES
    span = TYPES * GROUP
    wz = step * TYPES // 8
    turn_of = step % (8 // TYPES)
    low = pl.ds(pl.multiple_of(step * span, span), span)
    high = pl.ds(pl.multiple_of(1152 + turn_of * span, span), span)
    sides = ((send_w, halo_w), (send_e, halo_e))

    def project():
        channel = lax.broadcasted_iota(jnp.int32, (1, 128), 1)
        scale = LOG2E / math.sqrt(32.0)
        heads = [jnp.where((channel >= 32 * i) & (channel < 32 * i + 32), scale, 0.0) for i in range(3)]
        own, halo = (
            jnp.concatenate([jnp.concatenate([s[k][low, :], s[k][high, :]], axis=1) for s in sides], axis=0)
            for k in range(2)
        )
        return heads, mm(own, weight[wz]), mm(halo, weight[wz, :, 256:])

    def score(heads, own_qkv, halo_kv):
        scores, values = [], []
        ones = jnp.ones((16, 144), BF16)
        for s in range(2):
            for t in range(TYPES):
                at = span * s + GROUP * t
                parts = [own_qkv[at : at + GROUP, 256:], halo_kv[at : at + GROUP]]
                pair_kv = jnp.concatenate(parts[::-1] if s == 0 else parts, axis=0)
                keys = pair_kv[:, :256].astype(BF16)
                turned = pair_kv[:, 256:].T.astype(BF16)
                flags = jnp.where(wz == 1, 1, 0) + (
                    jnp.where(turn_of == 8 // TYPES - 1, 2, 0) if t == TYPES - 1 else 0
                )
                bad = (codes[0] & flags) != 0
                place = codes[1]
                for g in range(2):
                    q = own_qkv[at : at + GROUP, 128 * g : 128 * g + 128]
                    queries = jnp.concatenate([q * heads[i] for i in range(3)] + [jnp.zeros((40, 128), F32)], axis=0)
                    raw = mm(keys[:, 128 * g : 128 * g + 128], queries.astype(BF16), NT)
                    rows = pl.ds(step * TYPES + t, 24, stride=16)
                    table = [
                        jnp.concatenate([tables[m, 2 * g + k, rows, :] for k in range(2)], axis=1)
                        for m in (3 - s, 2 - s, 6 - s, 5 - s)
                    ]
                    chunks = []
                    for c in range(6):
                        u, v = divmod(2 * c, 6)
                        offset = turn(jnp.where(place < GROUP - 12 * v, table[u], table[2 + u]), 12 * v)
                        chunks.append(jnp.where(bad, NEG, raw[24 * c : 24 * c + 24] + offset))
                    scores.append(jnp.concatenate(chunks, axis=0))
                    values.append(jnp.concatenate([turned[128 * g : 128 * g + 96], ones], axis=0))
        return scores, values

    def soften(scores):
        return [jnp.exp2(x - jnp.max(x, axis=0, keepdims=True)).astype(BF16) for x in scores]

    def keep(mixes):
        for n in range(2 * TYPES):
            pieces = []
            for g in range(2):
                mixed = mixes[2 * n + g]
                inverse = 1.0 / mixed[96:97]
                for i in range(3):
                    at = GROUP * i
                    pieces.append(mixed[32 * i : 32 * i + 32, at : at + GROUP] * inverse[:, at : at + GROUP])
            held[GROUP * n : GROUP * n + GROUP, :] = jnp.concatenate(pieces, axis=0).T
        for s in range(2):
            ref = sides[s][0]
            upper = pltpu.roll(ref[high, :].astype(F32), 64 * wz, 1)
            kept[span * s : span * s + span, :] = jnp.concatenate(
                [ref[low, :].astype(F32), upper[:, :64]], axis=1
            )

    def attend():
        return mm(held[...].astype(BF16), wp[...]).astype(BF16).astype(F32)

    def join(attended):
        middle = (kept[...] + gain1[...] * norm(attended, 1e-05)).astype(BF16)
        return middle, mm(middle, w_in[...])

    def feed(hidden):
        twice = (hidden * (1.0 + lax.erf(hidden * (1.0 / math.sqrt(2.0))))).astype(BF16)
        return mm(twice, w_out[...])

    def finish(middle, reduced2):
        result = (middle.astype(F32) + gain2[...] * norm(reduced2, 4e-05)).astype(BF16)
        before = (step + 8 // TYPES - 1) % (8 // TYPES)
        for s in range(2):
            done[s, pl.ds(pl.multiple_of(before * span, span), span), :] = result[span * s : span * s + span]

    @pl.when(step == 0)
    def _():
        scores, values = score(*project())
        weights = soften(scores)
        keep([mm(v, w) for v, w in zip(values, weights)])

    @pl.when((step > 0) & (step < steps))
    def _():
        attended = attend()
        projected = project()
        middle, hidden = join(attended)
        scores, values = score(*projected)
        reduced2 = feed(hidden)
        weights = soften(scores)
        mixes = [mm(v, w) for v, w in zip(values, weights)]
        finish(middle, reduced2)
        keep(mixes)

    @pl.when(step == steps)
    def _():
        middle, hidden = join(attend())
        finish(middle, feed(hidden))

    @pl.when((step == steps // 2) | (step == steps))
    def _():
        for half in range(2):
            for j in range(3):
                pairs = TILE_PAIRS[j]
                if j == 0:
                    rows = jnp.concatenate([done[half, 432:576, :], done[half, 0:288, :]], axis=0)
                else:
                    rows = done[half, 144 * pairs[0] : 144 * pairs[0] + 288, :]
                back = mm(unmat[j, :, : 144 * len(pairs)], rows).astype(BF16)
                for c in range(6):
                    for level in range(2):
                        k = 2 * c + level
                        z = lax.rem(2 * step // (steps // 2) + 3 + level, 4)
                        out[z, 6 * half + c, 16 * j : 16 * j + 16, :] = back[16 * k : 16 * k + 16]


def shifted_by(value, axis, steps):
    count = lax.axis_size(axis)
    return lax.ppermute(value, axis, [(i, (i + steps) % count) for i in range(count)])


def per_device(
    tokens, qkv_weight, proj_weight, bias_table, bias_index, norm_gain1, norm_gain2, mlp_in, mlp_out
):
    levels, lat, strip, channels = tokens.shape
    types, heads, count = bias_table.shape
    tok = tokens.transpose(0, 2, 1, 3)
    vmem = pl.BlockSpec(memory_space=pltpu.VMEM)
    send_shape = jax.ShapeDtypeStruct((types * GROUP * 3 // 2, 128), BF16)

    send_w, send_e = pl.pallas_call(
        pack_kernel,
        out_shape=(send_shape, send_shape),
        in_specs=[vmem] * 2,
        out_specs=(vmem,) * 2,
        name="pack",
    )(tok, jnp.asarray(pack_matrices(), BF16))
    halo_w = shifted_by(send_e, "lon", 1)
    table = bias_table.transpose(1, 0, 2).reshape(heads * types, count)
    tables, weight, w_out = pl.pallas_call(
        gather_kernel,
        out_shape=(
            jax.ShapeDtypeStruct((7, LANES // 128, 384, 128), F32),
            jax.ShapeDtypeStruct((2, 256, 768), BF16),
            jax.ShapeDtypeStruct(mlp_out.shape, BF16),
        ),
        in_specs=[vmem] * 4,
        out_specs=(vmem,) * 3,
        scratch_shapes=[
            pltpu.VMEM((3328, 128), F32),
            pltpu.VMEM((12, 4, GROUP, 128), F32),
            pltpu.VMEM((24, 144), jnp.int32),
            pltpu.SMEM((24, 144), jnp.int32),
            pltpu.SemaphoreType.DMA,
        ],
        compiler_params=pltpu.CompilerParams(vmem_limit_bytes=16 * 1024 * 1024),
        cost_estimate=pl.CostEstimate(flops=6_000_000_000, bytes_accessed=4_000_000, transcendentals=0),
        name="bias_gather",
    )(table, bias_index, qkv_weight, mlp_out.T)
    halo_e = shifted_by(send_w, "lon", -1)
    out = pl.pallas_call(
        main_kernel,
        grid=(types // TYPES + 1,),
        out_shape=jax.ShapeDtypeStruct((levels, strip, lat, channels), BF16),
        in_specs=[vmem] * 13,
        out_specs=vmem,
        scratch_shapes=[
            pltpu.VMEM((2, 576, channels), BF16),
            pltpu.VMEM((2 * TYPES * GROUP, channels), F32),
            pltpu.VMEM((2 * TYPES * GROUP, channels), F32),
        ],
        compiler_params=pltpu.CompilerParams(vmem_limit_bytes=32 * 1024 * 1024),
        name="block",
    )(
        send_w,
        send_e,
        halo_w,
        halo_e,
        tables,
        jnp.asarray(mask_codes(), jnp.int32),
        weight,
        proj_weight,
        norm_gain1[None],
        norm_gain2[None],
        mlp_in,
        w_out,
        jnp.asarray(unpack_matrices(), BF16),
    )
    return out.transpose(0, 2, 1, 3)


def solution(mesh):
    placed = (P("grp", None, "lon", None), P(), P(), P(), P(), P(), P(), P(), P())
    return jax.shard_map(
        per_device,
        mesh=mesh,
        in_specs=placed,
        out_specs=P("grp", None, "lon", None),
        check_vma=False,
    )
```

time: 72.5 us -> 36.4 us (0.50)
  Pallas kernels: 48.7 us -> 27 us
  local copies, waits for them, and re-layouts: 17.8 us -> 1.9 us
  waiting for transfers between devices: 0.01 us -> 1.8 us
    pallas_call x3, Pallas kernels: 48.7 us -> 27 us  [the longest x1 17 us: per_device(): pl.pallas_call(main_kernel, grid=(types // TYPES + 1,), out_shape=jax.Sha...]
    unnamed x32 -> x24, local copies, waits for them, and re-layouts: 11.9 us -> 1.9 us
    pallas_call x2 -> x0, local copies, waits for them, and re-layouts: 3.21 us -> none  [per_device(): pl.pallas_call(pack_kernel, out_shape=(half_shape, half_shape), in_specs=...]
    ppermute x2 -> x0, local copies, waits for them, and re-layouts: 2.6 us -> none  [shifted_by(): lax.ppermute(value, axis, [(i, (i + steps) % count) for i in range(count)])]
    ppermute x2, waiting for transfers between devices: 0.01 us -> 1.8 us  [shifted_by(): lax.ppermute(value, axis, [(i, (i + steps) % count) for i in range(count)])]
  transfers between devices with their start and end apart: 2 -> 2, of which waited for: 0 -> 1; matrix products, arithmetic and copies ran while one was open for 5% -> 0% of each run, Pallas kernels for 25% -> 19%
where the time goes in v2:
time: 36.4 us; the launch traced here: 36.3 us
  Pallas kernels  27 us (74%)
  starting transfers between devices  5.44 us (15%)
  local copies, waits for them, and re-layouts  1.9 us (5%)
  waiting for transfers between devices  1.8 us (5%)
    pallas_call x1, Pallas kernels, per_device(): pl.pallas_call(main_kernel, grid=(types // TYPES + 1,), out_shape=jax.Sha...  17 us
    pallas_call x1, Pallas kernels, per_device(): pl.pallas_call(gather_kernel, out_shape=(jax.ShapeDtypeStruct((7, LANES /...  6.89 us
    ppermute x2, starting transfers between devices, shifted_by(): lax.ppermute(value, axis, [(i, (i + steps) % count) for i in range(count)])  5.44 us
    pallas_call x1, Pallas kernels, per_device(): pl.pallas_call(pack_kernel, out_shape=(send_shape, send_shape), in_specs=...  3.11 us
    unnamed x24, local copies, waits for them, and re-layouts  1.9 us
    ppermute x2, waiting for transfers between devices, shifted_by(): lax.ppermute(value, axis, [(i, (i + steps) % count) for i in range(count)])  1.8 us
  transfers between devices with their start and end apart: 2, of which 1 were waited for; matrix products, arithmetic and copies ran while one was open for 0% of the time, Pallas kernels for 19%

profile of v2, /device:TPU:0, one launch (start us, length us, event | category | flops | bytes accessed | tf_op | source)
XLA Modules:
  0.0 36.3 jit_solution(16175425570159129966)
XLA Ops:
  0.0 0.0 copy-start.9
  0.0 0.0 copy-start.8
  0.0 3.1 %pack.1 = (bf16[1728,128]{1,0:T(8,128)(2,1)}, bf16[1728,128]{1,0:T(8,128)(2,1)}) custom-call(bf16[4,12,48,192]{3,2,1,0:T(8,128)(2,1)} %bitcast.12, bf16[7,144,192]{2,1,0:T(8,128)(2,1)} %constant.6.clone.mats), custom_call_target="tpu_custom_call" | custom-call | tf_op jit(solution)/shard_map/pack/pallas_call | solution.py:327
  3.1 5.4 %collective-permute-start.1 = (bf16[1728,128]{1,0:T(8,128)(2,1)}, bf16[1728,128]{1,0:T(8,128)(2,1)S(1)}, u32[]{:S(2)}, u32[]{:S(2)}) collective-permute-start(bf16[1728,128]{1,0:T(8,128)(2,1)} %get-tuple-element.10.send_w), channel_id=1, source_target_pairs={{0,15},{1,0},{2,1},{3,2},{4,3},{5,4},{6,5},{7,6},{8,7},{9,8},{10,9... | collective-permute-start | bytes 1327112 | tf_op jit(solution)/shard_map/ppermute | solution.py:315
  8.6 0.0 collective-permute-start
  8.6 0.0 copy-done.9
  8.6 0.0 copy-done.8
  8.6 0.0 copy-start.10
  8.6 0.9 %copy-done.10 = bf16[192,576]{1,0:T(8,128)(2,1)S(1)} copy-done((bf16[192,576]{1,0:T(8,128)(2,1)S(1)}, bf16[192,576]{1,0:T(8,128)(2,1)}, u32[]{:S(2)}) %copy-start.10) | copy-done | bytes 221208
  9.5 0.0 copy-start.11
  9.5 0.9 %copy-done.11 = s32[144,144]{1,0:T(8,128)S(1)} copy-done((s32[144,144]{1,0:T(8,128)S(1)}, s32[144,144]{1,0:T(8,128)}, u32[]{:S(2)}) %copy-start.11) | copy-done | bytes 82968
  10.4 0.0 copy-start
  10.4 0.0 copy-start.1
  10.4 0.0 copy-start.2
  10.4 0.0 copy-start.3
  10.4 0.0 copy-start.4
  10.4 0.0 copy-start.5
  10.5 0.0 copy-start.6
  10.5 0.0 copy-start.7
  10.5 6.9 %bias_gather.1 = (f32[7,4,384,128]{3,2,1,0:T(8,128)S(1)}, bf16[2,256,768]{2,1,0:T(8,128)(2,1)S(1)}, bf16[768,192]{1,0:T(8,128)(2,1)S(1)}) custom-call(f32[96,3312]{1,0:T(8,128)S(1)} %bitcast.10, s32[144,144]{1,0:T(8,128)S(1)} %copy-done.11, bf16[192,576]{1,0:T(8,128)(2,1)S(1)} %copy-done.10, bf16[192,768]{1,0:T(8,128)(2,1)S(1)} %bitcast.11), custom_call_target="tpu_custom_call" | custom-call | flops 6000000000 | bytes 4000000 | tf_op jit(solution)/shard_map/bias_gather/pallas_call | solution.py:336
  17.4 0.0 collective-permute-done.1.halo_e
  17.4 1.8 %collective-permute-done.halo_w = bf16[1728,128]{1,0:T(8,128)(2,1)S(1)} collective-permute-done((bf16[1728,128]{1,0:T(8,128)(2,1)}, bf16[1728,128]{1,0:T(8,128)(2,1)S(1)}, u32[]{:S(2)}, u32[]{:S(2)}) %collective-permute-start) | collective-permute-done | bytes 442400 | tf_op jit(solution)/shard_map/ppermute | solution.py:315
  19.2 0.0 copy-done
  19.2 0.0 copy-done.1
  19.2 0.0 copy-done.2
  19.2 0.0 copy-done.3
  19.2 0.0 copy-done.4
  19.2 0.0 copy-done.5
  19.2 0.0 copy-done.6
  19.2 0.0 copy-done.7
  19.3 17.0 %block.1 = bf16[4,12,48,192]{3,2,1,0:T(8,128)(2,1)} custom-call(bf16[1728,128]{1,0:T(8,128)(2,1)S(1)} %copy-done.1, bf16[1728,128]{1,0:T(8,128)(2,1)S(1)} %copy-done.2, bf16[1728,128]{1,0:T(8,128)(2,1)S(1)} %collective-permute-done.halo_w, bf16[1728,128]{1,0:T(8,128)(2,1)S(1)} %collective-permute-done.1.halo_e, ...), custom_call_target="tpu_custom_call" | custom-call | tf_op jit(solution)/shard_map/block/pallas_call | solution.py:357
Async XLA Ops:
  0.0 8.6 %copy-start.9 = (bf16[768,192]{0,1:T(8,128)(2,1)S(1)}, bf16[768,192]{0,1:T(8,128)(2,1)}, u32[]{:S(2)}) copy-start(bf16[768,192]{0,1:T(8,128)(2,1)} %param.20) | copy-start | bytes 884740
  0.0 8.6 %copy-start.8 = (f32[16,6,3312]{2,0,1:T(8,128)S(1)}, f32[16,6,3312]{2,0,1:T(8,128)}, u32[]{:S(2)}) copy-start(f32[16,6,3312]{2,0,1:T(8,128)} %param.15) | copy-start | bytes 3815428
  3.1 14.3 %collective-permute-start.1 = (bf16[1728,128]{1,0:T(8,128)(2,1)}, bf16[1728,128]{1,0:T(8,128)(2,1)S(1)}, u32[]{:S(2)}, u32[]{:S(2)}) collective-permute-start(bf16[1728,128]{1,0:T(8,128)(2,1)} %get-tuple-element.10.send_w), channel_id=1, source_target_pairs={{0,15},{1,0},{2,1},{3,2},{4,3},{5,4},{6,5},{7,6},{8,7},{9,8},{10,9... | collective-permute-start | bytes 1327112 | tf_op jit(solution)/shard_map/ppermute | solution.py:315
  8.6 10.6 %collective-permute-start = (bf16[1728,128]{1,0:T(8,128)(2,1)}, bf16[1728,128]{1,0:T(8,128)(2,1)S(1)}, u32[]{:S(2)}, u32[]{:S(2)}) collective-permute-start(bf16[1728,128]{1,0:T(8,128)(2,1)} %get-tuple-element.11.send_e), channel_id=1, source_target_pairs={{0,1},{1,2},{2,3},{3,4},{4,5},{5,6},{6,7},{7,8},{8,9},{9,10},{10,1... | collective-permute-start | bytes 1327112 | tf_op jit(solution)/shard_map/ppermute | solution.py:315
  8.6 0.9 %copy-start.10 = (bf16[192,576]{1,0:T(8,128)(2,1)S(1)}, bf16[192,576]{1,0:T(8,128)(2,1)}, u32[]{:S(2)}) copy-start(bf16[192,576]{1,0:T(8,128)(2,1)} %qkv.1) | copy-start | bytes 663556
  9.5 0.9 %copy-start.11 = (s32[144,144]{1,0:T(8,128)S(1)}, s32[144,144]{1,0:T(8,128)}, u32[]{:S(2)}) copy-start(s32[144,144]{1,0:T(8,128)} %index.1) | copy-start | bytes 248836
  10.4 8.8 %copy-start = (bf16[3,192,432]{2,1,0:T(8,128)(2,1)S(1)}, bf16[3,192,432]{2,1,0:T(8,128)(2,1)}, u32[]{:S(2)}) copy-start(bf16[3,192,432]{2,1,0:T(8,128)(2,1)} %constant.8.clone.unmat) | copy-start | bytes 1492996
  10.4 8.8 %copy-start.1 = (bf16[1728,128]{1,0:T(8,128)(2,1)S(1)}, bf16[1728,128]{1,0:T(8,128)(2,1)}, u32[]{:S(2)}) copy-start(bf16[1728,128]{1,0:T(8,128)(2,1)} %get-tuple-element.10.send_w) | copy-start | bytes 1327108
  10.4 8.8 %copy-start.2 = (bf16[1728,128]{1,0:T(8,128)(2,1)S(1)}, bf16[1728,128]{1,0:T(8,128)(2,1)}, u32[]{:S(2)}) copy-start(bf16[1728,128]{1,0:T(8,128)(2,1)} %get-tuple-element.11.send_e) | copy-start | bytes 1327108
  10.4 8.8 %copy-start.3 = (bf16[192,768]{1,0:T(8,128)(2,1)S(1)}, bf16[192,768]{1,0:T(8,128)(2,1)}, u32[]{:S(2)}) copy-start(bf16[192,768]{1,0:T(8,128)(2,1)} %w_in.1) | copy-start | bytes 884740
  10.4 8.8 %copy-start.4 = (bf16[192,192]{1,0:T(8,128)(2,1)S(1)}, bf16[192,192]{1,0:T(8,128)(2,1)}, u32[]{:S(2)}) copy-start(bf16[192,192]{1,0:T(8,128)(2,1)} %wp.1) | copy-start | bytes 221188
  10.4 8.8 %copy-start.5 = (s32[2,24,256]{2,1,0:T(8,128)S(1)}, s32[2,24,256]{2,1,0:T(8,128)}, u32[]{:S(2)}) copy-start(s32[2,24,256]{2,1,0:T(8,128)} %constant.7.clone.codes) | copy-start | bytes 147460
  10.5 8.8 %copy-start.6 = (f32[192]{0:T(256)S(1)}, f32[192]{0:T(256)}, u32[]{:S(2)}) copy-start(f32[192]{0:T(256)} %param.17) | copy-start | bytes 2308
  10.5 8.8 %copy-start.7 = (f32[192]{0:T(256)S(1)}, f32[192]{0:T(256)}, u32[]{:S(2)}) copy-start(f32[192]{0:T(256)} %param.18) | copy-start | bytes 2308

commit v3 on v2

--- a/solution.py
+++ b/solution.py
@@ -103,7 +103,7 @@
     return jnp.concatenate([pltpu.roll(x[:, k : k + half], by % half, 1) for k in range(0, x.shape[1], half)], axis=1)
 
 
-def gather_kernel(tab, index, qkv, mlp_out_t, tables, weight, w_out, tab_t, rows, picked, idx, sem):
+def gather_kernel(tab, index, qkv, mlp_out_t, codes, bias, weight, w_out, tables, tab_t, rows, picked, idx, sem):
     numbers = index[...].astype(F32)
     turned = numbers.T
     picked[...] = jnp.concatenate(
@@ -169,6 +169,22 @@
         return carry
 
     lax.fori_loop(0, 12, variants, 0)
+    place = jnp.concatenate([codes[1], codes[1]], axis=1)
+
+    def widen(t, carry):
+        mine = [
+            jnp.concatenate([tables[m, k, pl.ds(t, 24, stride=16), :] for k in range(LANES // 128)], axis=1)
+            for m in range(7)
+        ]
+        for s in range(2):
+            for c in range(6):
+                u, v = divmod(2 * c, 6)
+                m = 3 - s - u
+                first = pl.multiple_of(t * 288 + s * 144 + 24 * c, 8)
+                bias[pl.ds(first, 24), :] = turn(jnp.where(place < GROUP - 12 * v, mine[m], mine[3 + m]), 12 * v)
+        return carry
+
+    lax.fori_loop(0, 16, widen, 0)
 
 
 def norm(values, eps):
@@ -179,7 +195,7 @@
 
 
 def main_kernel(
-    send_w, send_e, halo_w, halo_e, tables, codes, weight, wp, gain1, gain2, w_in, w_out, unmat, out, done, held, kept
+    send_w, send_e, halo_w, halo_e, bias, codes, weight, wp, gain1, gain2, w_in, w_out, unmat, out, done, held, kept
 ):
     step = pl.program_id(0)
     steps = 16 // TYPES
@@ -200,52 +216,61 @@
         )
         return heads, mm(own, weight[wz]), mm(halo, weight[wz, :, 256:])
 
-    def score(heads, own_qkv, halo_kv):
-        scores, values = [], []
-        ones = jnp.ones((16, 144), BF16)
-        for s in range(2):
-            for t in range(TYPES):
-                at = span * s + GROUP * t
-                parts = [own_qkv[at : at + GROUP, 256:], halo_kv[at : at + GROUP]]
-                pair_kv = jnp.concatenate(parts[::-1] if s == 0 else parts, axis=0)
-                keys = pair_kv[:, :256].astype(BF16)
-                turned = pair_kv[:, 256:].T.astype(BF16)
-                flags = jnp.where(wz == 1, 1, 0) + (
-                    jnp.where(turn_of == 8 // TYPES - 1, 2, 0) if t == TYPES - 1 else 0
-                )
-                bad = (codes[0] & flags) != 0
-                place = codes[1]
-                for g in range(2):
-                    q = own_qkv[at : at + GROUP, 128 * g : 128 * g + 128]
-                    queries = jnp.concatenate([q * heads[i] for i in range(3)] + [jnp.zeros((40, 128), F32)], axis=0)
-                    raw = mm(keys[:, 128 * g : 128 * g + 128], queries.astype(BF16), NT)
-                    rows = pl.ds(step * TYPES + t, 24, stride=16)
-                    table = [
-                        jnp.concatenate([tables[m, 2 * g + k, rows, :] for k in range(2)], axis=1)
-                        for m in (3 - s, 2 - s, 6 - s, 5 - s)
-                    ]
-                    chunks = []
-                    for c in range(6):
-                        u, v = divmod(2 * c, 6)
-                        offset = turn(jnp.where(place < GROUP - 12 * v, table[u], table[2 + u]), 12 * v)
-                        chunks.append(jnp.where(bad, NEG, raw[24 * c : 24 * c + 24] + offset))
-                    scores.append(jnp.concatenate(chunks, axis=0))
-                    values.append(jnp.concatenate([turned[128 * g : 128 * g + 96], ones], axis=0))
-        return scores, values
+    chains = [(s, t) for s in range(2) for t in range(TYPES)]
+
+    def queries_of(heads, own_qkv):
+        out = []
+        for s, t in chains:
+            at = span * s + GROUP * t
+            for g in range(2):
+                q = own_qkv[at : at + GROUP, 128 * g : 128 * g + 128]
+                blocks = [q * heads[i] for i in range(3)] + [jnp.zeros((40, 128), F32)]
+                out.append(jnp.concatenate(blocks, axis=0).astype(BF16))
+        return out
+
+    def windows(own_qkv, halo_kv, lanes):
+        out = []
+        for s, t in chains:
+            at = span * s + GROUP * t
+            parts = [own_qkv[at : at + GROUP, 256:][:, lanes], halo_kv[at : at + GROUP, lanes]]
+            out.append(jnp.concatenate(parts[::-1] if s == 0 else parts, axis=0))
+        return out
+
+    def score(keys, queries):
+        out = []
+        for n, (s, t) in enumerate(chains):
+            flags = jnp.where(wz == 1, 1, 0) + (jnp.where(turn_of == 8 // TYPES - 1, 2, 0) if t == TYPES - 1 else 0)
+            bad = (codes[0] & flags) != 0
+            for g in range(2):
+                raw = mm(keys[n][:, 128 * g : 128 * g + 128], queries[2 * n + g], NT)
+                chunks = []
+                for k in range(6):
+                    first = pl.multiple_of((step * TYPES + t) * 288 + s * 144 + 24 * k, 8)
+                    offset = bias[pl.ds(first, 24), 256 * g : 256 * g + 256]
+                    chunks.append(jnp.where(bad, NEG, raw[24 * k : 24 * k + 24] + offset))
+                out.append(jnp.concatenate(chunks, axis=0))
+        return out
 
     def soften(scores):
         return [jnp.exp2(x - jnp.max(x, axis=0, keepdims=True)).astype(BF16) for x in scores]
 
+    def mix(turned, weights):
+        ones = jnp.ones((16, 144), BF16)
+        return [
+            mm(jnp.concatenate([turned[n // 2][128 * (n % 2) : 128 * (n % 2) + 96], ones], axis=0), weights[n])
+            for n in range(4 * TYPES)
+        ]
+
     def keep(mixes):
+        scaled = []
+        for mixed in mixes:
+            inverse = 1.0 / mixed[96:97]
+            scaled.append([mixed[32 * i : 32 * i + 32] * inverse for i in range(3)])
+        moved = [
+            jnp.concatenate([p[i][:, GROUP * i : GROUP * i + GROUP] for i in range(3)], axis=0) for p in scaled
+        ]
         for n in range(2 * TYPES):
-            pieces = []
-            for g in range(2):
-                mixed = mixes[2 * n + g]
-                inverse = 1.0 / mixed[96:97]
-                for i in range(3):
-                    at = GROUP * i
-                    pieces.append(mixed[32 * i : 32 * i + 32, at : at + GROUP] * inverse[:, at : at + GROUP])
-            held[GROUP * n : GROUP * n + GROUP, :] = jnp.concatenate(pieces, axis=0).T
+            held[GROUP * n : GROUP * n + GROUP, :] = jnp.concatenate(moved[2 * n : 2 * n + 2], axis=0).T
         for s in range(2):
             ref = sides[s][0]
             upper = pltpu.roll(ref[high, :].astype(F32), 64 * wz, 1)
@@ -254,37 +279,44 @@
             )
 
     def attend():
-        return mm(held[...].astype(BF16), wp[...]).astype(BF16).astype(F32)
+        return mm(held[...].astype(BF16), wp[...])
 
     def join(attended):
-        middle = (kept[...] + gain1[...] * norm(attended, 1e-05)).astype(BF16)
-        return middle, mm(middle, w_in[...])
+        middle = kept[...] + gain1[...] * norm(attended, 1e-05)
+        return middle, mm(middle.astype(BF16), w_in[...])
 
     def feed(hidden):
         twice = (hidden * (1.0 + lax.erf(hidden * (1.0 / math.sqrt(2.0))))).astype(BF16)
         return mm(twice, w_out[...])
 
     def finish(middle, reduced2):
-        result = (middle.astype(F32) + gain2[...] * norm(reduced2, 4e-05)).astype(BF16)
+        result = (middle + gain2[...] * norm(reduced2, 4e-05)).astype(BF16)
         before = (step + 8 // TYPES - 1) % (8 // TYPES)
         for s in range(2):
             done[s, pl.ds(pl.multiple_of(before * span, span), span), :] = result[span * s : span * s + span]
 
+    keyed, valued = slice(0, 256), slice(256, 512)
+
     @pl.when(step == 0)
     def _():
-        scores, values = score(*project())
-        weights = soften(scores)
-        keep([mm(v, w) for v, w in zip(values, weights)])
+        heads, own_qkv, halo_kv = project()
+        keys = [x.astype(BF16) for x in windows(own_qkv, halo_kv, keyed)]
+        scores = score(keys, queries_of(heads, own_qkv))
+        turned = [x.T.astype(BF16) for x in windows(own_qkv, halo_kv, valued)]
+        keep(mix(turned, soften(scores)))
 
     @pl.when((step > 0) & (step < steps))
     def _():
         attended = attend()
-        projected = project()
+        heads, own_qkv, halo_kv = project()
         middle, hidden = join(attended)
-        scores, values = score(*projected)
         reduced2 = feed(hidden)
+        keys = [x.astype(BF16) for x in windows(own_qkv, halo_kv, keyed)]
+        queries = queries_of(heads, own_qkv)
+        scores = score(keys, queries)
+        turned = [x.T.astype(BF16) for x in windows(own_qkv, halo_kv, valued)]
         weights = soften(scores)
-        mixes = [mm(v, w) for v, w in zip(values, weights)]
+        mixes = mix(turned, weights)
         finish(middle, reduced2)
         keep(mixes)
 
@@ -332,17 +364,19 @@
         name="pack",
     )(tok, jnp.asarray(pack_matrices(), BF16))
     halo_w = shifted_by(send_e, "lon", 1)
+    codes = jnp.asarray(mask_codes(), jnp.int32)
     table = bias_table.transpose(1, 0, 2).reshape(heads * types, count)
-    tables, weight, w_out = pl.pallas_call(
+    bias, weight, w_out = pl.pallas_call(
         gather_kernel,
         out_shape=(
-            jax.ShapeDtypeStruct((7, LANES // 128, 384, 128), F32),
+            jax.ShapeDtypeStruct((types * 288, LANES), F32),
             jax.ShapeDtypeStruct((2, 256, 768), BF16),
             jax.ShapeDtypeStruct(mlp_out.shape, BF16),
         ),
-        in_specs=[vmem] * 4,
+        in_specs=[vmem] * 5,
         out_specs=(vmem,) * 3,
         scratch_shapes=[
+            pltpu.VMEM((7, LANES // 128, 384, 128), F32),
             pltpu.VMEM((3328, 128), F32),
             pltpu.VMEM((12, 4, GROUP, 128), F32),
             pltpu.VMEM((24, 144), jnp.int32),
@@ -352,7 +386,7 @@
         compiler_params=pltpu.CompilerParams(vmem_limit_bytes=16 * 1024 * 1024),
         cost_estimate=pl.CostEstimate(flops=6_000_000_000, bytes_accessed=4_000_000, transcendentals=0),
         name="bias_gather",
-    )(table, bias_index, qkv_weight, mlp_out.T)
+    )(table, bias_index, qkv_weight, mlp_out.T, codes)
     halo_e = shifted_by(send_w, "lon", -1)
     out = pl.pallas_call(
         main_kernel,
@@ -365,15 +399,15 @@
             pltpu.VMEM((2 * TYPES * GROUP, channels), F32),
             pltpu.VMEM((2 * TYPES * GROUP, channels), F32),
         ],
-        compiler_params=pltpu.CompilerParams(vmem_limit_bytes=32 * 1024 * 1024),
+        compiler_params=pltpu.CompilerParams(vmem_limit_bytes=16 * 1024 * 1024),
         name="block",
     )(
         send_w,
         send_e,
         halo_w,
         halo_e,
-        tables,
-        jnp.asarray(mask_codes(), jnp.int32),
+        bias,
+        codes,
         weight,
         proj_weight,
         norm_gain1[None],

time: 36.4 us -> 35.2 us (0.967)
  waiting for transfers between devices: 1.8 us -> 0.01 us
  Pallas kernels: 27 us -> 27.5 us
    pallas_call x1, Pallas kernels: 6.89 us -> 10.7 us  [per_device(): pl.pallas_call(gather_kernel, out_shape=(jax.ShapeDtypeStruct((types * 28...]
    pallas_call x1, Pallas kernels: 17 us -> 13.7 us  [per_device(): pl.pallas_call(main_kernel, grid=(types // TYPES + 1,), out_shape=jax.Sha...]
    ppermute x2, waiting for transfers between devices: 1.8 us -> 0.01 us  [shifted_by(): lax.ppermute(value, axis, [(i, (i + steps) % count) for i in range(count)])]
  transfers between devices with their start and end apart: 2 -> 2, of which waited for: 1 -> 0; matrix products, arithmetic and copies ran while one was open for 0% -> 0% of each run, Pallas kernels for 19% -> 31%
where the time goes in v3:
time: 35.2 us; the launch traced here: 35 us
  Pallas kernels  27.5 us (78%)
  starting transfers between devices  5.46 us (16%)
  local copies, waits for them, and re-layouts  1.89 us (5%)
    pallas_call x1, Pallas kernels, per_device(): pl.pallas_call(main_kernel, grid=(types // TYPES + 1,), out_shape=jax.Sha...  13.7 us
    pallas_call x1, Pallas kernels, per_device(): pl.pallas_call(gather_kernel, out_shape=(jax.ShapeDtypeStruct((types * 28...  10.7 us
    ppermute x2, starting transfers between devices, shifted_by(): lax.ppermute(value, axis, [(i, (i + steps) % count) for i in range(count)])  5.46 us
    pallas_call x1, Pallas kernels, per_device(): pl.pallas_call(pack_kernel, out_shape=(send_shape, send_shape), in_specs=...  3.11 us
    unnamed x24, local copies, waits for them, and re-layouts  1.89 us
  transfers between devices with their start and end apart: 2, of which 0 were waited for; matrix products, arithmetic and copies ran while one was open for 0% of the time, Pallas kernels for 31%

profile of v3, /device:TPU:0, one launch (start us, length us, event | category | flops | bytes accessed | tf_op | source)
XLA Modules:
  0.0 35.0 jit_solution(1392039478441733832)
XLA Ops:
  0.0 0.0 copy-start.5
  0.0 0.0 copy-start.9
  0.0 0.0 copy-start.8
  0.0 3.1 %pack.1 = (bf16[1728,128]{1,0:T(8,128)(2,1)}, bf16[1728,128]{1,0:T(8,128)(2,1)}) custom-call(bf16[4,12,48,192]{3,2,1,0:T(8,128)(2,1)} %bitcast.12, bf16[7,144,192]{2,1,0:T(8,128)(2,1)} %constant.6.clone.mats), custom_call_target="tpu_custom_call" | custom-call | tf_op jit(solution)/shard_map/pack/pallas_call | solution.py:359
  3.1 5.5 %collective-permute-start.1 = (bf16[1728,128]{1,0:T(8,128)(2,1)}, bf16[1728,128]{1,0:T(8,128)(2,1)S(1)}, u32[]{:S(2)}, u32[]{:S(2)}) collective-permute-start(bf16[1728,128]{1,0:T(8,128)(2,1)} %get-tuple-element.10.send_w), channel_id=1, source_target_pairs={{0,15},{1,0},{2,1},{3,2},{4,3},{5,4},{6,5},{7,6},{8,7},{9,8},{10,9... | collective-permute-start | bytes 1327112 | tf_op jit(solution)/shard_map/ppermute | solution.py:347
  8.6 0.0 collective-permute-start
  8.6 0.0 copy-done.5
  8.6 0.0 copy-done.9
  8.6 0.0 copy-done.8
  8.6 0.0 copy-start.10
  8.6 0.9 %copy-done.10 = bf16[192,576]{1,0:T(8,128)(2,1)S(1)} copy-done((bf16[192,576]{1,0:T(8,128)(2,1)S(1)}, bf16[192,576]{1,0:T(8,128)(2,1)}, u32[]{:S(2)}) %copy-start.10) | copy-done | bytes 221208
  9.5 0.0 copy-start.11
  9.5 0.9 %copy-done.11 = s32[144,144]{1,0:T(8,128)S(1)} copy-done((s32[144,144]{1,0:T(8,128)S(1)}, s32[144,144]{1,0:T(8,128)}, u32[]{:S(2)}) %copy-start.11) | copy-done | bytes 82968
  10.4 0.0 copy-start
  10.4 0.0 copy-start.1
  10.5 0.0 copy-start.2
  10.5 0.0 copy-start.3
  10.5 0.0 copy-start.4
  10.5 0.0 copy-start.6
  10.5 0.0 copy-start.7
  10.5 10.7 %bias_gather.1 = (f32[4608,512]{1,0:T(8,128)S(1)}, bf16[2,256,768]{2,1,0:T(8,128)(2,1)S(1)}, bf16[768,192]{1,0:T(8,128)(2,1)S(1)}) custom-call(f32[96,3312]{1,0:T(8,128)S(1)} %bitcast.10, s32[144,144]{1,0:T(8,128)S(1)} %copy-done.11, bf16[192,576]{1,0:T(8,128)(2,1)S(1)} %copy-done.10, bf16[192,768]{1,0:T(8,128)(2,1)S(1)} %bitcast.11, s32[2,24,256]{2,1,0:T(8,128)S(1)} %copy-done.5), custom_call_target="tpu_custom_call" | custom-call | flops 6000000000 | bytes 4000000 | tf_op jit(solution)/shard_map/bias_gather/pallas_call | solution.py:369
  21.2 0.0 collective-permute-done.1.halo_e
  21.2 0.0 collective-permute-done.halo_w
  21.2 0.0 copy-done
  21.2 0.0 copy-done.1
  21.2 0.0 copy-done.2
  21.2 0.0 copy-done.3
  21.3 0.0 copy-done.4
  21.3 0.0 copy-done.6
  21.3 0.0 copy-done.7
  21.3 13.7 %block.1 = bf16[4,12,48,192]{3,2,1,0:T(8,128)(2,1)} custom-call(bf16[1728,128]{1,0:T(8,128)(2,1)S(1)} %copy-done.1, bf16[1728,128]{1,0:T(8,128)(2,1)S(1)} %copy-done.2, bf16[1728,128]{1,0:T(8,128)(2,1)S(1)} %collective-permute-done.halo_w, bf16[1728,128]{1,0:T(8,128)(2,1)S(1)} %collective-permute-done.1.halo_e, f32[4608,512]{1,0:T(8,128)S(1)} %get-tuple-element.12.bias, ...), custom_call_target="tpu_custom_call" | custom-call | tf_op jit(solution)/shard_map/block/pallas_call | solution.py:391
Async XLA Ops:
  0.0 8.6 %copy-start.5 = (s32[2,24,256]{2,1,0:T(8,128)S(1)}, s32[2,24,256]{2,1,0:T(8,128)}, u32[]{:S(2)}) copy-start(s32[2,24,256]{2,1,0:T(8,128)} %constant.7.clone.codes) | copy-start | bytes 147460
  0.0 8.6 %copy-start.9 = (bf16[768,192]{0,1:T(8,128)(2,1)S(1)}, bf16[768,192]{0,1:T(8,128)(2,1)}, u32[]{:S(2)}) copy-start(bf16[768,192]{0,1:T(8,128)(2,1)} %param.20) | copy-start | bytes 884740
  0.0 8.6 %copy-start.8 = (f32[16,6,3312]{2,0,1:T(8,128)S(1)}, f32[16,6,3312]{2,0,1:T(8,128)}, u32[]{:S(2)}) copy-start(f32[16,6,3312]{2,0,1:T(8,128)} %param.15) | copy-start | bytes 3815428
  3.1 18.1 %collective-permute-start.1 = (bf16[1728,128]{1,0:T(8,128)(2,1)}, bf16[1728,128]{1,0:T(8,128)(2,1)S(1)}, u32[]{:S(2)}, u32[]{:S(2)}) collective-permute-start(bf16[1728,128]{1,0:T(8,128)(2,1)} %get-tuple-element.10.send_w), channel_id=1, source_target_pairs={{0,15},{1,0},{2,1},{3,2},{4,3},{5,4},{6,5},{7,6},{8,7},{9,8},{10,9... | collective-permute-start | bytes 1327112 | tf_op jit(solution)/shard_map/ppermute | solution.py:347
  8.6 12.6 %collective-permute-start = (bf16[1728,128]{1,0:T(8,128)(2,1)}, bf16[1728,128]{1,0:T(8,128)(2,1)S(1)}, u32[]{:S(2)}, u32[]{:S(2)}) collective-permute-start(bf16[1728,128]{1,0:T(8,128)(2,1)} %get-tuple-element.11.send_e), channel_id=1, source_target_pairs={{0,1},{1,2},{2,3},{3,4},{4,5},{5,6},{6,7},{7,8},{8,9},{9,10},{10,1... | collective-permute-start | bytes 1327112 | tf_op jit(solution)/shard_map/ppermute | solution.py:347
  8.6 0.9 %copy-start.10 = (bf16[192,576]{1,0:T(8,128)(2,1)S(1)}, bf16[192,576]{1,0:T(8,128)(2,1)}, u32[]{:S(2)}) copy-start(bf16[192,576]{1,0:T(8,128)(2,1)} %qkv.1) | copy-start | bytes 663556
  9.5 0.9 %copy-start.11 = (s32[144,144]{1,0:T(8,128)S(1)}, s32[144,144]{1,0:T(8,128)}, u32[]{:S(2)}) copy-start(s32[144,144]{1,0:T(8,128)} %index.1) | copy-start | bytes 248836
  10.4 10.8 %copy-start = (bf16[3,192,432]{2,1,0:T(8,128)(2,1)S(1)}, bf16[3,192,432]{2,1,0:T(8,128)(2,1)}, u32[]{:S(2)}) copy-start(bf16[3,192,432]{2,1,0:T(8,128)(2,1)} %constant.8.clone.unmat) | copy-start | bytes 1492996
  10.4 10.8 %copy-start.1 = (bf16[1728,128]{1,0:T(8,128)(2,1)S(1)}, bf16[1728,128]{1,0:T(8,128)(2,1)}, u32[]{:S(2)}) copy-start(bf16[1728,128]{1,0:T(8,128)(2,1)} %get-tuple-element.10.send_w) | copy-start | bytes 1327108
  10.5 10.8 %copy-start.2 = (bf16[1728,128]{1,0:T(8,128)(2,1)S(1)}, bf16[1728,128]{1,0:T(8,128)(2,1)}, u32[]{:S(2)}) copy-start(bf16[1728,128]{1,0:T(8,128)(2,1)} %get-tuple-element.11.send_e) | copy-start | bytes 1327108
  10.5 10.8 %copy-start.3 = (bf16[192,768]{1,0:T(8,128)(2,1)S(1)}, bf16[192,768]{1,0:T(8,128)(2,1)}, u32[]{:S(2)}) copy-start(bf16[192,768]{1,0:T(8,128)(2,1)} %w_in.1) | copy-start | bytes 884740
  10.5 10.8 %copy-start.4 = (bf16[192,192]{1,0:T(8,128)(2,1)S(1)}, bf16[192,192]{1,0:T(8,128)(2,1)}, u32[]{:S(2)}) copy-start(bf16[192,192]{1,0:T(8,128)(2,1)} %wp.1) | copy-start | bytes 221188
  10.5 10.8 %copy-start.6 = (f32[192]{0:T(256)S(1)}, f32[192]{0:T(256)}, u32[]{:S(2)}) copy-start(f32[192]{0:T(256)} %param.17) | copy-start | bytes 2308
  10.5 10.8 %copy-start.7 = (f32[192]{0:T(256)S(1)}, f32[192]{0:T(256)}, u32[]{:S(2)}) copy-start(f32[192]{0:T(256)} %param.18) | copy-start | bytes 2308

commit v4 on v3

--- a/solution.py
+++ b/solution.py
@@ -14,7 +14,7 @@
 NN = (((1,), (0,)), ((), ()))
 HEADS = 6
 GROUP = 72
-TYPES = 4
+TYPES = 8
 LANES = 512
 F32 = jnp.float32
 BF16 = jnp.bfloat16
@@ -168,7 +168,7 @@
                     tables[n, k, at, :] = value[:, 128 * k : 128 * k + 128]
         return carry
 
-    lax.fori_loop(0, 12, variants, 0)
+    lax.fori_loop(0, 12, variants, 0, unroll=4)
     place = jnp.concatenate([codes[1], codes[1]], axis=1)
 
     def widen(t, carry):
@@ -184,7 +184,7 @@
                 bias[pl.ds(first, 24), :] = turn(jnp.where(place < GROUP - 12 * v, mine[m], mine[3 + m]), 12 * v)
         return carry
 
-    lax.fori_loop(0, 16, widen, 0)
+    lax.fori_loop(0, 16, widen, 0, unroll=8)
 
 
 def norm(values, eps):

time: 35.2 us -> 34.1 us (0.969)
  Pallas kernels: 27.5 us -> 26.4 us
    pallas_call x1, Pallas kernels: 10.7 us -> 9.85 us  [per_device(): pl.pallas_call(gather_kernel, out_shape=(jax.ShapeDtypeStruct((types * 28...]
  transfers between devices with their start and end apart: 2 -> 2, of which waited for: 0 -> 0; matrix products, arithmetic and copies ran while one was open for 0% -> 0% of each run, Pallas kernels for 31% -> 29%
where the time goes in v4:
time: 34.1 us; the launch traced here: 33.9 us
  Pallas kernels  26.4 us (77%)
  starting transfers between devices  5.46 us (16%)
  local copies, waits for them, and re-layouts  1.89 us (6%)
    pallas_call x1, Pallas kernels, per_device(): pl.pallas_call(main_kernel, grid=(types // TYPES + 1,), out_shape=jax.Sha...  13.4 us
    pallas_call x1, Pallas kernels, per_device(): pl.pallas_call(gather_kernel, out_shape=(jax.ShapeDtypeStruct((types * 28...  9.85 us
    ppermute x2, starting transfers between devices, shifted_by(): lax.ppermute(value, axis, [(i, (i + steps) % count) for i in range(count)])  5.46 us
    pallas_call x1, Pallas kernels, per_device(): pl.pallas_call(pack_kernel, out_shape=(send_shape, send_shape), in_specs=...  3.11 us
    unnamed x24, local copies, waits for them, and re-layouts  1.89 us
  transfers between devices with their start and end apart: 2, of which 0 were waited for; matrix products, arithmetic and copies ran while one was open for 0% of the time, Pallas kernels for 29%

profile of v4, /device:TPU:0, one launch (start us, length us, event | category | flops | bytes accessed | tf_op | source)
XLA Modules:
  0.0 33.9 jit_solution(4808326445416743434)
XLA Ops:
  0.0 0.0 copy-start.5
  0.0 0.0 copy-start.9
  0.0 0.0 copy-start.8
  0.0 3.1 %pack.1 = (bf16[1728,128]{1,0:T(8,128)(2,1)}, bf16[1728,128]{1,0:T(8,128)(2,1)}) custom-call(bf16[4,12,48,192]{3,2,1,0:T(8,128)(2,1)} %bitcast.12, bf16[7,144,192]{2,1,0:T(8,128)(2,1)} %constant.6.clone.mats), custom_call_target="tpu_custom_call" | custom-call | tf_op jit(solution)/shard_map/pack/pallas_call | solution.py:359
  3.1 5.5 %collective-permute-start.1 = (bf16[1728,128]{1,0:T(8,128)(2,1)}, bf16[1728,128]{1,0:T(8,128)(2,1)S(1)}, u32[]{:S(2)}, u32[]{:S(2)}) collective-permute-start(bf16[1728,128]{1,0:T(8,128)(2,1)} %get-tuple-element.10.send_w), channel_id=1, source_target_pairs={{0,15},{1,0},{2,1},{3,2},{4,3},{5,4},{6,5},{7,6},{8,7},{9,8},{10,9... | collective-permute-start | bytes 1327112 | tf_op jit(solution)/shard_map/ppermute | solution.py:347
  8.6 0.0 collective-permute-start
  8.6 0.0 copy-done.5
  8.6 0.0 copy-done.9
  8.6 0.0 copy-done.8
  8.6 0.0 copy-start.10
  8.6 0.9 %copy-done.10 = bf16[192,576]{1,0:T(8,128)(2,1)S(1)} copy-done((bf16[192,576]{1,0:T(8,128)(2,1)S(1)}, bf16[192,576]{1,0:T(8,128)(2,1)}, u32[]{:S(2)}) %copy-start.10) | copy-done | bytes 221208
  9.5 0.0 copy-start.11
  9.5 0.9 %copy-done.11 = s32[144,144]{1,0:T(8,128)S(1)} copy-done((s32[144,144]{1,0:T(8,128)S(1)}, s32[144,144]{1,0:T(8,128)}, u32[]{:S(2)}) %copy-start.11) | copy-done | bytes 82968
  10.4 0.0 copy-start
  10.5 0.0 copy-start.1
  10.5 0.0 copy-start.2
  10.5 0.0 copy-start.3
  10.5 0.0 copy-start.4
  10.5 0.0 copy-start.6
  10.5 0.0 copy-start.7
  10.5 9.9 %bias_gather.1 = (f32[4608,512]{1,0:T(8,128)S(1)}, bf16[2,256,768]{2,1,0:T(8,128)(2,1)S(1)}, bf16[768,192]{1,0:T(8,128)(2,1)S(1)}) custom-call(f32[96,3312]{1,0:T(8,128)S(1)} %bitcast.10, s32[144,144]{1,0:T(8,128)S(1)} %copy-done.11, bf16[192,576]{1,0:T(8,128)(2,1)S(1)} %copy-done.10, bf16[192,768]{1,0:T(8,128)(2,1)S(1)} %bitcast.11, s32[2,24,256]{2,1,0:T(8,128)S(1)} %copy-done.5), custom_call_target="tpu_custom_call" | custom-call | flops 6000000000 | bytes 4000000 | tf_op jit(solution)/shard_map/bias_gather/pallas_call | solution.py:369
  20.4 0.0 collective-permute-done.1.halo_e
  20.4 0.0 collective-permute-done.halo_w
  20.4 0.0 copy-done
  20.4 0.0 copy-done.1
  20.4 0.0 copy-done.2
  20.4 0.0 copy-done.3
  20.4 0.0 copy-done.4
  20.4 0.0 copy-done.6
  20.4 0.0 copy-done.7
  20.4 13.4 %block.1 = bf16[4,12,48,192]{3,2,1,0:T(8,128)(2,1)} custom-call(bf16[1728,128]{1,0:T(8,128)(2,1)S(1)} %copy-done.1, bf16[1728,128]{1,0:T(8,128)(2,1)S(1)} %copy-done.2, bf16[1728,128]{1,0:T(8,128)(2,1)S(1)} %collective-permute-done.halo_w, bf16[1728,128]{1,0:T(8,128)(2,1)S(1)} %collective-permute-done.1.halo_e, f32[4608,512]{1,0:T(8,128)S(1)} %get-tuple-element.12.bias, ...), custom_call_target="tpu_custom_call" | custom-call | tf_op jit(solution)/shard_map/block/pallas_call | solution.py:391
Async XLA Ops:
  0.0 8.6 %copy-start.5 = (s32[2,24,256]{2,1,0:T(8,128)S(1)}, s32[2,24,256]{2,1,0:T(8,128)}, u32[]{:S(2)}) copy-start(s32[2,24,256]{2,1,0:T(8,128)} %constant.7.clone.codes) | copy-start | bytes 147460
  0.0 8.6 %copy-start.9 = (bf16[768,192]{0,1:T(8,128)(2,1)S(1)}, bf16[768,192]{0,1:T(8,128)(2,1)}, u32[]{:S(2)}) copy-start(bf16[768,192]{0,1:T(8,128)(2,1)} %param.20) | copy-start | bytes 884740
  0.0 8.6 %copy-start.8 = (f32[16,6,3312]{2,0,1:T(8,128)S(1)}, f32[16,6,3312]{2,0,1:T(8,128)}, u32[]{:S(2)}) copy-start(f32[16,6,3312]{2,0,1:T(8,128)} %param.15) | copy-start | bytes 3815428
  3.1 17.2 %collective-permute-start.1 = (bf16[1728,128]{1,0:T(8,128)(2,1)}, bf16[1728,128]{1,0:T(8,128)(2,1)S(1)}, u32[]{:S(2)}, u32[]{:S(2)}) collective-permute-start(bf16[1728,128]{1,0:T(8,128)(2,1)} %get-tuple-element.10.send_w), channel_id=1, source_target_pairs={{0,15},{1,0},{2,1},{3,2},{4,3},{5,4},{6,5},{7,6},{8,7},{9,8},{10,9... | collective-permute-start | bytes 1327112 | tf_op jit(solution)/shard_map/ppermute | solution.py:347
  8.6 11.8 %collective-permute-start = (bf16[1728,128]{1,0:T(8,128)(2,1)}, bf16[1728,128]{1,0:T(8,128)(2,1)S(1)}, u32[]{:S(2)}, u32[]{:S(2)}) collective-permute-start(bf16[1728,128]{1,0:T(8,128)(2,1)} %get-tuple-element.11.send_e), channel_id=1, source_target_pairs={{0,1},{1,2},{2,3},{3,4},{4,5},{5,6},{6,7},{7,8},{8,9},{9,10},{10,1... | collective-permute-start | bytes 1327112 | tf_op jit(solution)/shard_map/ppermute | solution.py:347
  8.6 0.9 %copy-start.10 = (bf16[192,576]{1,0:T(8,128)(2,1)S(1)}, bf16[192,576]{1,0:T(8,128)(2,1)}, u32[]{:S(2)}) copy-start(bf16[192,576]{1,0:T(8,128)(2,1)} %qkv.1) | copy-start | bytes 663556
  9.5 0.9 %copy-start.11 = (s32[144,144]{1,0:T(8,128)S(1)}, s32[144,144]{1,0:T(8,128)}, u32[]{:S(2)}) copy-start(s32[144,144]{1,0:T(8,128)} %index.1) | copy-start | bytes 248836
  10.4 9.9 %copy-start = (bf16[3,192,432]{2,1,0:T(8,128)(2,1)S(1)}, bf16[3,192,432]{2,1,0:T(8,128)(2,1)}, u32[]{:S(2)}) copy-start(bf16[3,192,432]{2,1,0:T(8,128)(2,1)} %constant.8.clone.unmat) | copy-start | bytes 1492996
  10.5 9.9 %copy-start.1 = (bf16[1728,128]{1,0:T(8,128)(2,1)S(1)}, bf16[1728,128]{1,0:T(8,128)(2,1)}, u32[]{:S(2)}) copy-start(bf16[1728,128]{1,0:T(8,128)(2,1)} %get-tuple-element.10.send_w) | copy-start | bytes 1327108
  10.5 9.9 %copy-start.2 = (bf16[1728,128]{1,0:T(8,128)(2,1)S(1)}, bf16[1728,128]{1,0:T(8,128)(2,1)}, u32[]{:S(2)}) copy-start(bf16[1728,128]{1,0:T(8,128)(2,1)} %get-tuple-element.11.send_e) | copy-start | bytes 1327108
  10.5 10.0 %copy-start.3 = (bf16[192,768]{1,0:T(8,128)(2,1)S(1)}, bf16[192,768]{1,0:T(8,128)(2,1)}, u32[]{:S(2)}) copy-start(bf16[192,768]{1,0:T(8,128)(2,1)} %w_in.1) | copy-start | bytes 884740
  10.5 10.0 %copy-start.4 = (bf16[192,192]{1,0:T(8,128)(2,1)S(1)}, bf16[192,192]{1,0:T(8,128)(2,1)}, u32[]{:S(2)}) copy-start(bf16[192,192]{1,0:T(8,128)(2,1)} %wp.1) | copy-start | bytes 221188
  10.5 10.0 %copy-start.6 = (f32[192]{0:T(256)S(1)}, f32[192]{0:T(256)}, u32[]{:S(2)}) copy-start(f32[192]{0:T(256)} %param.17) | copy-start | bytes 2308
  10.5 10.0 %copy-start.7 = (f32[192]{0:T(256)S(1)}, f32[192]{0:T(256)}, u32[]{:S(2)}) copy-start(f32[192]{0:T(256)} %param.18) | copy-start | bytes 2308

commit v5 on v4

--- a/solution.py
+++ b/solution.py
@@ -73,7 +73,7 @@
     return np.stack([code, place])
 
 
-def pack_kernel(tok, mats, send_w, send_e):
+def pack_kernel(tok, mats, index, qkv, send_w, send_e, picked, weight):
     for wz in range(2):
         zs = ((2 * wz + 1) % 4, (2 * wz + 2) % 4)
         for half, send in ((0, send_w), (1, send_e)):
@@ -94,24 +94,11 @@
                 first = 576 * wz + 144 * pair
                 send[first : first + 144, :] = piece[:, :128]
                 send[1152 + 144 * pair : 1296 + 144 * pair, 64 * wz : 64 * wz + 64] = piece[:, 128:]
-
-
-def turn(x, by):
-    half = LANES // 2
-    if by % half == 0:
-        return x
-    return jnp.concatenate([pltpu.roll(x[:, k : k + half], by % half, 1) for k in range(0, x.shape[1], half)], axis=1)
-
-
-def gather_kernel(tab, index, qkv, mlp_out_t, codes, bias, weight, w_out, tables, tab_t, rows, picked, idx, sem):
     numbers = index[...].astype(F32)
     turned = numbers.T
     picked[...] = jnp.concatenate(
         [numbers[12 * e : 12 * e + 1] for e in range(12)] + [turned[12 * e : 12 * e + 1] for e in range(12)], axis=0
     ).astype(jnp.int32)
-    copy = pltpu.make_async_copy(picked, idx, sem)
-    copy.start()
-    w_out[...] = mlp_out_t[...].astype(F32).T.astype(BF16)
     whole = qkv[...].astype(F32)
     gap = jnp.zeros((192, 32), F32)
     cols = []
@@ -123,6 +110,19 @@
         weight[wz, 0:128, :] = wide[:128]
         weight[wz, 128 + 64 * wz : 192 + 64 * wz, :] = wide[128:]
         weight[wz, 192 - 64 * wz : 256 - 64 * wz, :] = none
+
+
+def turn(x, by):
+    half = LANES // 2
+    if by % half == 0:
+        return x
+    return jnp.concatenate([pltpu.roll(x[:, k : k + half], by % half, 1) for k in range(0, x.shape[1], half)], axis=1)
+
+
+def gather_kernel(tab, picked, mlp_out_t, codes, bias, w_out, tables, tab_t, rows, idx, sem):
+    copy = pltpu.make_async_copy(picked, idx, sem)
+    copy.start()
+    w_out[...] = mlp_out_t[...].astype(F32).T.astype(BF16)
     count = tab.shape[1]
     for k in range(0, count, 128):
         n = min(128, count - k)
@@ -356,37 +356,40 @@
     vmem = pl.BlockSpec(memory_space=pltpu.VMEM)
     send_shape = jax.ShapeDtypeStruct((types * GROUP * 3 // 2, 128), BF16)
 
-    send_w, send_e = pl.pallas_call(
+    send_w, send_e, picked, weight = pl.pallas_call(
         pack_kernel,
-        out_shape=(send_shape, send_shape),
-        in_specs=[vmem] * 2,
-        out_specs=(vmem,) * 2,
+        out_shape=(
+            send_shape,
+            send_shape,
+            jax.ShapeDtypeStruct((24, 144), jnp.int32),
+            jax.ShapeDtypeStruct((2, 256, 768), BF16),
+        ),
+        in_specs=[vmem] * 4,
+        out_specs=(vmem,) * 4,
         name="pack",
-    )(tok, jnp.asarray(pack_matrices(), BF16))
+    )(tok, jnp.asarray(pack_matrices(), BF16), bias_index, qkv_weight)
     halo_w = shifted_by(send_e, "lon", 1)
     codes = jnp.asarray(mask_codes(), jnp.int32)
     table = bias_table.transpose(1, 0, 2).reshape(heads * types, count)
-    bias, weight, w_out = pl.pallas_call(
+    bias, w_out = pl.pallas_call(
         gather_kernel,
         out_shape=(
             jax.ShapeDtypeStruct((types * 288, LANES), F32),
-            jax.ShapeDtypeStruct((2, 256, 768), BF16),
             jax.ShapeDtypeStruct(mlp_out.shape, BF16),
         ),
-        in_specs=[vmem] * 5,
-        out_specs=(vmem,) * 3,
+        in_specs=[vmem] * 4,
+        out_specs=(vmem,) * 2,
         scratch_shapes=[
             pltpu.VMEM((7, LANES // 128, 384, 128), F32),
             pltpu.VMEM((3328, 128), F32),
             pltpu.VMEM((12, 4, GROUP, 128), F32),
-            pltpu.VMEM((24, 144), jnp.int32),
             pltpu.SMEM((24, 144), jnp.int32),
             pltpu.SemaphoreType.DMA,
         ],
         compiler_params=pltpu.CompilerParams(vmem_limit_bytes=16 * 1024 * 1024),
         cost_estimate=pl.CostEstimate(flops=6_000_000_000, bytes_accessed=4_000_000, transcendentals=0),
         name="bias_gather",
-    )(table, bias_index, qkv_weight, mlp_out.T, codes)
+    )(table, picked, mlp_out.T, codes)
     halo_e = shifted_by(send_w, "lon", -1)
     out = pl.pallas_call(
         main_kernel,

time: 34.1 us -> 33.3 us (0.977)
  local copies, waits for them, and re-layouts: 1.89 us -> 0.78 us
  waiting for transfers between devices: 0.01 us -> 0.6 us
    unnamed x24, local copies, waits for them, and re-layouts: 1.89 us -> 0.78 us
    pallas_call x1, Pallas kernels: 9.85 us -> 9.2 us  [per_device(): pl.pallas_call(gather_kernel, out_shape=(jax.ShapeDtypeStruct((types * 28...]
    ppermute x2, waiting for transfers between devices: 0.01 us -> 0.6 us  [shifted_by(): lax.ppermute(value, axis, [(i, (i + steps) % count) for i in range(count)])]
    pallas_call x1, Pallas kernels: 3.11 us -> 3.48 us  [per_device(): pl.pallas_call(pack_kernel, out_shape=(send_shape, send_shape, jax.ShapeD...]
  transfers between devices with their start and end apart: 2 -> 2, of which waited for: 0 -> 1; matrix products, arithmetic and copies ran while one was open for 0% -> 0% of each run, Pallas kernels for 29% -> 28%
where the time goes in v5:
time: 33.3 us; the launch traced here: 33.1 us
  Pallas kernels  26.1 us (78%)
  starting transfers between devices  5.46 us (16%)
  local copies, waits for them, and re-layouts  0.78 us (2%)
  waiting for transfers between devices  0.6 us (2%)
    pallas_call x1, Pallas kernels, per_device(): pl.pallas_call(main_kernel, grid=(types // TYPES + 1,), out_shape=jax.Sha...  13.4 us
    pallas_call x1, Pallas kernels, per_device(): pl.pallas_call(gather_kernel, out_shape=(jax.ShapeDtypeStruct((types * 28...  9.2 us
    ppermute x2, starting transfers between devices, shifted_by(): lax.ppermute(value, axis, [(i, (i + steps) % count) for i in range(count)])  5.46 us
    pallas_call x1, Pallas kernels, per_device(): pl.pallas_call(pack_kernel, out_shape=(send_shape, send_shape, jax.ShapeD...  3.48 us
    unnamed x24, local copies, waits for them, and re-layouts  0.78 us
  transfers between devices with their start and end apart: 2, of which 1 were waited for; matrix products, arithmetic and copies ran while one was open for 0% of the time, Pallas kernels for 28%

profile of v5, /device:TPU:0, one launch (start us, length us, event | category | flops | bytes accessed | tf_op | source)
XLA Modules:
  0.0 33.1 jit_solution(8299170972152920563)
XLA Ops:
  0.0 0.0 copy-start.6
  0.0 0.0 copy-start.10
  0.0 0.0 copy-start.9
  0.0 3.5 %pack.1 = (bf16[1728,128]{1,0:T(8,128)(2,1)}, bf16[1728,128]{1,0:T(8,128)(2,1)}, s32[24,144]{1,0:T(8,128)}, bf16[2,256,768]{2,1,0:T(8,128)(2,1)}) custom-call(bf16[4,12,48,192]{3,2,1,0:T(8,128)(2,1)} %bitcast.12, bf16[7,144,192]{2,1,0:T(8,128)(2,1)} %constant.6.clone.mats, s32[144,144]{1,0:T(8,128)} %index.1, bf16[192,576]{1,0:T(8,128)(2,1)} %qkv.1), custom_call_target="tpu_custom_call" | custom-call | tf_op jit(solution)/shard_map/pack/pallas_call | solution.py:359
  3.5 5.5 %collective-permute-start.1 = (bf16[1728,128]{1,0:T(8,128)(2,1)}, bf16[1728,128]{1,0:T(8,128)(2,1)S(1)}, u32[]{:S(2)}, u32[]{:S(2)}) collective-permute-start(bf16[1728,128]{1,0:T(8,128)(2,1)} %get-tuple-element.11.send_w), channel_id=1, source_target_pairs={{0,15},{1,0},{2,1},{3,2},{4,3},{5,4},{6,5},{7,6},{8,7},{9,8},{10,9... | collective-permute-start | bytes 1327112 | tf_op jit(solution)/shard_map/ppermute | solution.py:347
  8.9 0.0 collective-permute-start
  8.9 0.0 copy-done.6
  9.0 0.0 copy-done.10
  9.0 0.0 copy-done.9
  9.0 0.0 copy-start.11
  9.0 0.7 %copy-done.11 = s32[24,144]{1,0:T(8,128)S(1)} copy-done((s32[24,144]{1,0:T(8,128)S(1)}, s32[24,144]{1,0:T(8,128)}, u32[]{:S(2)}) %copy-start.11) | copy-done | bytes 13848
  9.7 0.0 copy-start
  9.7 0.0 copy-start.1
  9.7 0.0 copy-start.2
  9.7 0.0 copy-start.3
  9.7 0.0 copy-start.4
  9.7 0.0 copy-start.5
  9.7 0.0 copy-start.7
  9.8 0.0 copy-start.8
  9.8 9.2 %bias_gather.1 = (f32[4608,512]{1,0:T(8,128)S(1)}, bf16[768,192]{1,0:T(8,128)(2,1)S(1)}) custom-call(f32[96,3312]{1,0:T(8,128)S(1)} %bitcast.10, s32[24,144]{1,0:T(8,128)S(1)} %copy-done.11, bf16[192,768]{1,0:T(8,128)(2,1)S(1)} %bitcast.11, s32[2,24,256]{2,1,0:T(8,128)S(1)} %copy-done.6), custom_call_target="tpu_custom_call" | custom-call | flops 6000000000 | bytes 4000000 | tf_op jit(solution)/shard_map/bias_gather/pallas_call | solution.py:374
  19.0 0.0 collective-permute-done.1.halo_e
  19.0 0.6 %collective-permute-done.halo_w = bf16[1728,128]{1,0:T(8,128)(2,1)S(1)} collective-permute-done((bf16[1728,128]{1,0:T(8,128)(2,1)}, bf16[1728,128]{1,0:T(8,128)(2,1)S(1)}, u32[]{:S(2)}, u32[]{:S(2)}) %collective-permute-start) | collective-permute-done | bytes 442400 | tf_op jit(solution)/shard_map/ppermute | solution.py:347
  19.6 0.0 copy-done
  19.6 0.0 copy-done.1
  19.6 0.0 copy-done.2
  19.6 0.0 copy-done.3
  19.6 0.0 copy-done.4
  19.6 0.0 copy-done.5
  19.6 0.0 copy-done.7
  19.6 0.0 copy-done.8
  19.6 13.4 %block.1 = bf16[4,12,48,192]{3,2,1,0:T(8,128)(2,1)} custom-call(bf16[1728,128]{1,0:T(8,128)(2,1)S(1)} %copy-done.2, bf16[1728,128]{1,0:T(8,128)(2,1)S(1)} %copy-done.3, bf16[1728,128]{1,0:T(8,128)(2,1)S(1)} %collective-permute-done.halo_w, bf16[1728,128]{1,0:T(8,128)(2,1)S(1)} %collective-permute-done.1.halo_e, f32[4608,512]{1,0:T(8,128)S(1)} %get-tuple-element.14.bias, ...), custom_call_target="tpu_custom_call" | custom-call | tf_op jit(solution)/shard_map/block/pallas_call | solution.py:394
Async XLA Ops:
  0.0 9.0 %copy-start.6 = (s32[2,24,256]{2,1,0:T(8,128)S(1)}, s32[2,24,256]{2,1,0:T(8,128)}, u32[]{:S(2)}) copy-start(s32[2,24,256]{2,1,0:T(8,128)} %constant.7.clone.codes) | copy-start | bytes 147460
  0.0 9.0 %copy-start.10 = (bf16[768,192]{0,1:T(8,128)(2,1)S(1)}, bf16[768,192]{0,1:T(8,128)(2,1)}, u32[]{:S(2)}) copy-start(bf16[768,192]{0,1:T(8,128)(2,1)} %param.20) | copy-start | bytes 884740
  0.0 9.0 %copy-start.9 = (f32[16,6,3312]{2,0,1:T(8,128)S(1)}, f32[16,6,3312]{2,0,1:T(8,128)}, u32[]{:S(2)}) copy-start(f32[16,6,3312]{2,0,1:T(8,128)} %param.15) | copy-start | bytes 3815428
  3.5 15.5 %collective-permute-start.1 = (bf16[1728,128]{1,0:T(8,128)(2,1)}, bf16[1728,128]{1,0:T(8,128)(2,1)S(1)}, u32[]{:S(2)}, u32[]{:S(2)}) collective-permute-start(bf16[1728,128]{1,0:T(8,128)(2,1)} %get-tuple-element.11.send_w), channel_id=1, source_target_pairs={{0,15},{1,0},{2,1},{3,2},{4,3},{5,4},{6,5},{7,6},{8,7},{9,8},{10,9... | collective-permute-start | bytes 1327112 | tf_op jit(solution)/shard_map/ppermute | solution.py:347
  8.9 10.6 %collective-permute-start = (bf16[1728,128]{1,0:T(8,128)(2,1)}, bf16[1728,128]{1,0:T(8,128)(2,1)S(1)}, u32[]{:S(2)}, u32[]{:S(2)}) collective-permute-start(bf16[1728,128]{1,0:T(8,128)(2,1)} %get-tuple-element.12.send_e), channel_id=1, source_target_pairs={{0,1},{1,2},{2,3},{3,4},{4,5},{5,6},{6,7},{7,8},{8,9},{9,10},{10,1... | collective-permute-start | bytes 1327112 | tf_op jit(solution)/shard_map/ppermute | solution.py:347
  9.0 0.7 %copy-start.11 = (s32[24,144]{1,0:T(8,128)S(1)}, s32[24,144]{1,0:T(8,128)}, u32[]{:S(2)}) copy-start(s32[24,144]{1,0:T(8,128)} %get-tuple-element.13.picked) | copy-start | bytes 41476
  9.7 9.9 %copy-start = (bf16[2,256,768]{2,1,0:T(8,128)(2,1)S(1)}, bf16[2,256,768]{2,1,0:T(8,128)(2,1)}, u32[]{:S(2)}) copy-start(bf16[2,256,768]{2,1,0:T(8,128)(2,1)} %get-tuple-element.15.weight) | copy-start | bytes 2359300
  9.7 9.9 %copy-start.1 = (bf16[3,192,432]{2,1,0:T(8,128)(2,1)S(1)}, bf16[3,192,432]{2,1,0:T(8,128)(2,1)}, u32[]{:S(2)}) copy-start(bf16[3,192,432]{2,1,0:T(8,128)(2,1)} %constant.8.clone.unmat) | copy-start | bytes 1492996
  9.7 9.9 %copy-start.2 = (bf16[1728,128]{1,0:T(8,128)(2,1)S(1)}, bf16[1728,128]{1,0:T(8,128)(2,1)}, u32[]{:S(2)}) copy-start(bf16[1728,128]{1,0:T(8,128)(2,1)} %get-tuple-element.11.send_w) | copy-start | bytes 1327108
  9.7 9.9 %copy-start.3 = (bf16[1728,128]{1,0:T(8,128)(2,1)S(1)}, bf16[1728,128]{1,0:T(8,128)(2,1)}, u32[]{:S(2)}) copy-start(bf16[1728,128]{1,0:T(8,128)(2,1)} %get-tuple-element.12.send_e) | copy-start | bytes 1327108
  9.7 9.9 %copy-start.4 = (bf16[192,768]{1,0:T(8,128)(2,1)S(1)}, bf16[192,768]{1,0:T(8,128)(2,1)}, u32[]{:S(2)}) copy-start(bf16[192,768]{1,0:T(8,128)(2,1)} %w_in.1) | copy-start | bytes 884740
  9.7 9.9 %copy-start.5 = (bf16[192,192]{1,0:T(8,128)(2,1)S(1)}, bf16[192,192]{1,0:T(8,128)(2,1)}, u32[]{:S(2)}) copy-start(bf16[192,192]{1,0:T(8,128)(2,1)} %wp.1) | copy-start | bytes 221188
  9.7 9.9 %copy-start.7 = (f32[192]{0:T(256)S(1)}, f32[192]{0:T(256)}, u32[]{:S(2)}) copy-start(f32[192]{0:T(256)} %param.17) | copy-start | bytes 2308
  9.8 9.9 %copy-start.8 = (f32[192]{0:T(256)S(1)}, f32[192]{0:T(256)}, u32[]{:S(2)}) copy-start(f32[192]{0:T(256)} %param.18) | copy-start | bytes 2308
